TPU v7x, 512 devices: a whole 4x4x16 slice. The times are simulated.
512 devices in a mesh: lat: 16 (over y, z_hi, core), lon: 32 (over x, z_lo).
Axes of the slice: x: 4, y: 4, z: 16 (z_hi: 2, z_lo: 8; z = z_hi * 8 + z_lo), core: 2. Of those that a mesh axis runs over, the one named last changes fastest.
Arguments:
- queries: bfloat16 [48, 1440, 1024], P('lat', 'lon'), may hold values from -68 to 68
- keys: bfloat16 [48, 1440, 1024], P('lat', 'lon'), may hold values from -6 to 6
- values: bfloat16 [48, 1440, 1024], P('lat', 'lon'), may hold values from -6 to 6
- cotangent: bfloat16 [48, 1440, 1024], P('lat', 'lon'), may hold values from -6 to 6
- pair_list: int32 [48, 9], replicated, may hold values from -1 to 8, as said below
- quad_index: int32 [48], replicated, may hold values from 0 to 31
- quad_table: float32 [32], replicated, may hold values from 0.1 to 1
Outputs:
- attended: bfloat16 [48, 1440, 1024], P('lat', 'lon')
- grad_queries: bfloat16 [48, 1440, 1024], P('lat', 'lon')
- grad_keys: bfloat16 [48, 1440, 1024], P('lat', 'lon')
- grad_values: bfloat16 [48, 1440, 1024], P('lat', 'lon')
Inputs may be any that keep to these rules, and one draw needn't show every extreme that they name: `pair_list`: row r lists distinct codes in increasing order, then -1 in the remaining slots; code 4 (the query tile itself) is always listed, codes 1 and 7 are listed wherever the row they name lies inside 0 to 47, and no listed code names a row outside 0 to 47.
All inputs are finite; a program needn't handle non-finite values.
Results may differ from a plain program's by a relative error of at most 0.012.
The roundings to bfloat16 on the way count: a program that leaves them out, or rounds other values in their place, can miss the bound.
Values may be sent and summed in bfloat16 or wider, within the bound.
A program may use at most 64 MiB of HBM per device.

v0:
```python
import jax
import jax.numpy as jnp
from jax import lax
from jax.sharding import PartitionSpec as P

HEADS = 16
HEAD = 64
TILE = 45
NPAIR = 9


def extended(cells, sides, width):
    for axis, dim in sides:
        count = lax.axis_size(axis)
        head = lax.slice_in_dim(cells, 0, width, axis=dim)
        tail = lax.slice_in_dim(cells, cells.shape[dim] - width, cells.shape[dim], axis=dim)
        cells = jnp.concatenate(
            [
                lax.ppermute(tail, axis, [(i, (i + 1) % count) for i in range(count)]),
                cells,
                lax.ppermute(head, axis, [((i + 1) % count, i) for i in range(count)]),
            ],
            axis=dim,
        )
    return cells


def passed_along(block, axis, distance):
    devices = range(lax.axis_size(axis))
    route = [((i - distance) % len(devices), i) for i in devices]
    return lax.ppermute(block, axis, route)


def from_behind(value, axis, by):
    size = lax.axis_size(axis)
    pairs = [(i, i + by) for i in range(size) if 0 <= i + by < size]
    return lax.ppermute(value, axis, pairs)


def row_weights(quad_index, quad_table, row_ids):
    lat_count = quad_index.shape[0]
    pick_row = row_ids[:, None] == jnp.arange(lat_count, dtype=jnp.int32)[None, :]
    table_entry = jnp.sum(jnp.where(pick_row, quad_index[None, :], 0), axis=1)
    pick_entry = table_entry[:, None] == jnp.arange(quad_table.shape[0], dtype=jnp.int32)[None, :]
    return jnp.sum(jnp.where(pick_entry, quad_table[None, :], 0.0), axis=1)


def split_heads(tile_block):
    return tile_block.reshape(tile_block.shape[:-1] + (HEADS, HEAD))


def pair_scores(query_tile, key_tile):
    return jnp.einsum(
        "tqhd,tkhd->thqk", query_tile, key_tile, preferred_element_type=jnp.float32
    ) * HEAD ** (-0.5)


def pair_slopes(query_tile, grad_tile, key_tile, value_tile, weight, row_lse, row_delta):
    pair_probs = weight * jnp.exp(pair_scores(query_tile, key_tile) - row_lse[..., None])
    grad_probs = jnp.einsum(
        "tqhd,tkhd->thqk", grad_tile, value_tile, preferred_element_type=jnp.float32
    )
    slope_tile = (pair_probs * (grad_probs - row_delta[..., None])).astype(jnp.bfloat16)
    return (pair_probs.astype(jnp.bfloat16), slope_tile)


def on_device(queries, keys, values, cotangent, pair_list, quad_index, quad_table):
    row_count, lon_width, model_width = queries.shape
    tile_count = lon_width // TILE
    head_scale = HEAD ** (-0.5)
    first_row = lax.axis_index("lat") * row_count
    tile_shape = (row_count, tile_count, TILE, HEADS, HEAD)
    q_heads = queries.reshape(tile_shape)
    g_heads = cotangent.reshape(tile_shape)
    kv_tiles = jnp.stack([keys, values]).reshape(2, row_count, tile_count, TILE, model_width)
    kv_ext = extended(kv_tiles, (("lat", 1), ("lon", 2)), 1)
    ext_rows = first_row - 1 + jnp.arange(row_count + 2, dtype=jnp.int32)
    ext_weight = row_weights(quad_index, quad_table, ext_rows)
    own_codes = lax.dynamic_slice_in_dim(pair_list, first_row, row_count, 0)

    def key_block(lat_pos, lon_pos):
        kv_block = lax.dynamic_slice(
            kv_ext, (0, lat_pos, lon_pos, 0, 0), (2, 1, tile_count, TILE, model_width)
        )
        weight = lax.dynamic_index_in_dim(ext_weight, lat_pos, 0, keepdims=False)
        return (split_heads(kv_block[0, 0]), split_heads(kv_block[1, 0]), weight)

    attended_rows = []
    lse_rows = []
    for row_index in range(row_count):
        start_state = (
            jnp.full((tile_count, HEADS, TILE), -1e30, jnp.float32),
            jnp.zeros((tile_count, HEADS, TILE), jnp.float32),
            jnp.zeros((tile_count, HEADS, TILE, HEAD), jnp.float32),
        )

        def visit_slot(slot_index, state_carry, row_index=row_index):
            pair_code = own_codes[row_index, slot_index]

            def take_pair(state_carry):
                row_max, row_total, accumulated = state_carry
                key_tile, value_tile, weight = key_block(row_index + pair_code // 3, pair_code % 3)
                scores = pair_scores(q_heads[row_index], key_tile)
                new_max = jnp.maximum(row_max, jnp.max(scores, axis=-1))
                rescale = jnp.exp(row_max - new_max)
                shares = weight * jnp.exp(scores - new_max[..., None])
                row_total = row_total * rescale + jnp.sum(shares, axis=-1)
                accumulated = accumulated * rescale[..., None] + jnp.einsum(
                    "thqk,tkhd->thqd",
                    shares.astype(jnp.bfloat16),
                    value_tile,
                    preferred_element_type=jnp.float32,
                )
                return (new_max, row_total, accumulated)

            return lax.cond(pair_code >= 0, take_pair, lambda state_carry: state_carry, state_carry)

        row_max, row_total, accumulated = lax.fori_loop(0, NPAIR, visit_slot, start_state)
        normed = accumulated / row_total[..., None]
        attended_rows.append(
            normed.transpose(0, 2, 1, 3).reshape(tile_count, TILE, model_width).astype(jnp.bfloat16)
        )
        lse_rows.append(row_max + jnp.log(row_total))
    attended_tiles = jnp.stack(attended_rows)
    lse_all = jnp.stack(lse_rows)
    products = cotangent.reshape(row_count, tile_count, TILE, model_width).astype(
        jnp.float32
    ) * attended_tiles.astype(jnp.float32)
    delta_all = jnp.sum(products.reshape(tile_shape), axis=-1).transpose(0, 1, 3, 2)
    grad_ext = jnp.zeros((2, row_count + 2, tile_count + 2, TILE, model_width), jnp.float32)
    query_grad_ext = grad_ext
    grad_rows = []
    for row_index in range(row_count):
        start_state = (jnp.zeros((tile_count, TILE, HEADS, HEAD), jnp.float32), query_grad_ext)

        def visit_slot(slot_index, state_carry, row_index=row_index):
            pair_code = own_codes[row_index, slot_index]

            def take_pair(state_carry):
                dq_accum, grad_buffer = state_carry
                lat_pos = row_index + pair_code // 3
                lon_pos = pair_code % 3
                key_tile, value_tile, weight = key_block(lat_pos, lon_pos)
                query_tile = q_heads[row_index]
                grad_tile = g_heads[row_index]
                probs_b, slope_tile = pair_slopes(
                    query_tile,
                    grad_tile,
                    key_tile,
                    value_tile,
                    weight,
                    lse_all[row_index],
                    delta_all[row_index],
                )
                dq_accum = (
                    dq_accum
                    + jnp.einsum(
                        "thqk,tkhd->tqhd", slope_tile, key_tile, preferred_element_type=jnp.float32
                    )
                    * head_scale
                )
                key_part = (
                    jnp.einsum(
                        "thqk,tqhd->tkhd",
                        slope_tile,
                        query_tile,
                        preferred_element_type=jnp.float32,
                    )
                    * head_scale
                )
                value_part = jnp.einsum(
                    "thqk,tqhd->tkhd", probs_b, grad_tile, preferred_element_type=jnp.float32
                )
                both_parts = jnp.stack([key_part, value_part]).reshape(
                    2, 1, tile_count, TILE, model_width
                )
                corner_index = (0, lat_pos, lon_pos, 0, 0)
                previous = lax.dynamic_slice(grad_buffer, corner_index, both_parts.shape)
                grad_buffer = lax.dynamic_update_slice(
                    grad_buffer, previous + both_parts, corner_index
                )
                return (dq_accum, grad_buffer)

            return lax.cond(pair_code >= 0, take_pair, lambda state_carry: state_carry, state_carry)

        dq_accum, query_grad_ext = lax.fori_loop(0, NPAIR, visit_slot, start_state)
        grad_rows.append(dq_accum.reshape(tile_count, TILE, model_width).astype(jnp.bfloat16))
    dq_tiles = jnp.stack(grad_rows)
    east_rim = passed_along(
        query_grad_ext[:, :, tile_count + 1 :].astype(jnp.bfloat16), "lon", 1
    ).astype(jnp.float32)
    west_rim = passed_along(query_grad_ext[:, :, :1].astype(jnp.bfloat16), "lon", -1).astype(
        jnp.float32
    )
    middle = query_grad_ext[:, :, 1 : tile_count + 1]
    middle = middle.at[:, :, :1].add(east_rim).at[:, :, tile_count - 1 :].add(west_rim)
    north_rim = from_behind(middle[:, row_count + 1 :].astype(jnp.bfloat16), "lat", 1).astype(
        jnp.float32
    )
    south_rim = from_behind(middle[:, :1].astype(jnp.bfloat16), "lat", -1).astype(jnp.float32)
    own_grads = (
        middle[:, 1 : row_count + 1].at[:, :1].add(north_rim).at[:, row_count - 1 :].add(south_rim)
    )
    key_grads = own_grads[0].astype(jnp.bfloat16)
    value_grads = own_grads[1].astype(jnp.bfloat16)
    out_shape = (row_count, lon_width, model_width)
    return (
        attended_tiles.reshape(out_shape),
        dq_tiles.reshape(out_shape),
        key_grads.reshape(out_shape),
        value_grads.reshape(out_shape),
    )


def solution(mesh):
    placed = (
        P("lat", "lon", None),
        P("lat", "lon", None),
        P("lat", "lon", None),
        P("lat", "lon", None),
        P(),
        P(),
        P(),
    )
    return jax.shard_map(
        on_device,
        mesh=mesh,
        in_specs=placed,
        out_specs=(
            P("lat", "lon", None),
            P("lat", "lon", None),
            P("lat", "lon", None),
            P("lat", "lon", None),
        ),
        check_vma=False,
    )
```

profile of v0, /device:TPU:223, one launch (start us, length us, event | category | flops | bytes accessed | tf_op | source)
XLA Modules:
  0.0 613.2 jit_solution(8277258628616109698)
XLA Ops:
  1.8 9.4 %collective-permute-start = (bf16[2,1,1,45,1024]{4,3,1,0,2:T(8,128)(2,1)S(1)}, bf16[2,1,1,45,1024]{4,3,1,0,2:T(8,128)(2,1)S(1)}, u32[]{:S(2)}, u32[]{:S(2)}) collective-permute-start(bf16[2,1,1,45,1024]{4,3,1,0,2:T(8,128)(2,1)S(1)} %get-tuple-element.1591), channel_id=1, source_target_pairs={{0,32},{32,64},{64,96},{96,128},{128,160},{160,192},{192,224},{224... | collective-permute-start | bytes 552968 | tf_op jit(solution)/shard_map/ppermute | solution.py:19
  13.3 9.0 %collective-permute-done = bf16[2,1,1,45,1024]{4,3,1,0,2:T(8,128)(2,1)S(1)} collective-permute-done((bf16[2,1,1,45,1024]{4,3,1,0,2:T(8,128)(2,1)S(1)}, bf16[2,1,1,45,1024]{4,3,1,0,2:T(8,128)(2,1)S(1)}, u32[]{:S(2)}, u32[]{:S(2)}) %collective-permute-start) | collective-permute-done | bytes 184352 | tf_op jit(solution)/shard_map/ppermute | solution.py:19
  22.4 8.3 %collective-permute-done.1 = bf16[2,1,1,45,1024]{4,3,1,0,2:T(8,128)(2,1)S(1)} collective-permute-done((bf16[2,1,1,45,1024]{4,3,1,0,2:T(8,128)(2,1)S(1)}, bf16[2,1,1,45,1024]{4,3,1,0,2:T(8,128)(2,1)S(1)}, u32[]{:S(2)}, u32[]{:S(2)}) %collective-permute-start.1) | collective-permute-done | bytes 184352 | tf_op jit(solution)/shard_map/ppermute | solution.py:21
  39.6 17.8 %collective-permute-done.3 = bf16[2,5,1,45,1024]{4,0,3,2,1:T(2,128)(2,1)} collective-permute-done((bf16[2,5,1,45,1024]{4,0,3,2,1:T(2,128)(2,1)}, bf16[2,5,1,45,1024]{4,0,3,2,1:T(2,128)(2,1)}, u32[]{:S(2)}, u32[]{:S(2)}) %collective-permute-start.3) | collective-permute-done | bytes 921632 | tf_op jit(solution)/shard_map/ppermute | solution.py:21
  58.9 15.9 %collective-permute-done.2 = bf16[2,5,1,45,1024]{4,0,3,2,1:T(2,128)(2,1)} collective-permute-done((bf16[2,5,1,45,1024]{4,0,3,2,1:T(2,128)(2,1)}, bf16[2,5,1,45,1024]{4,0,3,2,1:T(2,128)(2,1)}, u32[]{:S(2)}, u32[]{:S(2)}) %collective-permute-start.2) | collective-permute-done | bytes 921632 | tf_op jit(solution)/shard_map/ppermute | solution.py:19
  79.0 50.3 %while.103 = (s32[]{:T(128)}, f32[1,16,45]{2,1,0:T(8,128)S(1)}, f32[1,16,45]{2,1,0:T(8,128)S(1)}, f32[1,16,45,64]{3,2,1,0:T(8,128)S(1)}, s32[3,9]{1,0:T(4,128)S(...) while((s32[]{:T(128)}, f32[1,16,45]{2,1,0:T(8,128)S(1)}, ...), condition=%wide.region_13.14_spmd, body=%wide.region_8.13_spmd.sunk | while | flops 8647944 | bytes 2014374 | solution.py:118
  80.2 5.7 conditional.13
  87.0 5.7 conditional.13
  93.9 5.7 conditional.13
  100.7 5.7 conditional.13
  107.6 5.7 conditional.13
  114.4 5.7 conditional.13
  121.3 5.7 conditional.13
  129.6 61.6 %while.104 = (s32[]{:T(128)}, f32[1,16,45]{2,1,0:T(8,128)S(1)}, f32[1,16,45]{2,1,0:T(8,128)S(1)}, f32[1,16,45,64]{3,2,1,0:T(8,128)S(1)}, s32[3,9]{1,0:T(4,128)S(...) while((s32[]{:T(128)}, f32[1,16,45]{2,1,0:T(8,128)S(1)}, ...), condition=%wide.region_19.20_spmd, body=%wide.region_14.19_spmd.sunk | while | flops 8647944 | bytes 2014374 | solution.py:118
  130.8 5.7 conditional.14
  137.7 5.7 conditional.14
  144.5 5.7 conditional.14
  151.4 5.7 conditional.14
  158.2 5.7 conditional.14
  165.1 5.7 conditional.14
  171.9 5.7 conditional.14
  178.7 5.7 conditional.14
  185.6 5.7 conditional.14
  191.6 56.0 %while.102 = (s32[]{:T(128)}, f32[1,16,45]{2,1,0:T(8,128)S(1)}, f32[1,16,45]{2,1,0:T(8,128)S(1)}, f32[1,16,45,64]{3,2,1,0:T(8,128)S(1)}, s32[3,9]{1,0:T(4,128)S(...) while((s32[]{:T(128)}, f32[1,16,45]{2,1,0:T(8,128)S(1)}, ...), condition=%wide.region_7.8_spmd, body=%wide.region_2.7_spmd.sunk | while | flops 8647943 | bytes 2014362 | solution.py:118
  192.8 5.7 conditional.12
  199.6 5.7 conditional.12
  206.5 5.7 conditional.12
  213.3 5.7 conditional.12
  220.2 5.7 conditional.12
  227.0 5.7 conditional.12
  233.8 5.7 conditional.12
  240.7 5.7 conditional.12
  254.1 79.5 %while.105 = (s32[]{:T(128)}, f32[1,45,16,64]{3,1,2,0:T(8,128)S(1)}, f32[2,5,3,45,1024]{4,0,3,2,1:T(2,128)}, s32[3,9]{1,0:T(4,128)S(1)}, bf16[2,5,3,45,1024]{4,3...) while((s32[]{:T(128)}, f32[1,45,16,64]{3,1,2,0:T(8,128)S(1)}, ...), condition=%wide.region_24.25_spmd, body=%wide.region_21.24_spmd.sunk | while | flops 21285384 | bytes 6567150 | solution.py:186
  255.3 8.6 %conditional.15 = ((f32[1,45,16,64]{3,1,2,0:T(8,128)S(1)}, f32[2,5,3,45,1024]{4,0,3,2,1:T(2,128)})) conditional(s32[]{:T(128)} %convert_element_type.321, (f32[1,45,16,64]{3,1,2,0:T(8,128)S(1)}, f32[2,5,3,45,1024]{4,0,3,2,1:T(2,128)}) %tuple.267, (s32[]{:T(128)}, bf16[2,5,3,45,1024]{4,3,2,1,0:T(8,128)(2,1)}, f32[5]{0:T(128)S(1)}, ...), branch_computations={%region_22.22_spmd, %region_23.23_spmd} | conditional | flops 21285380 | bytes 6566911 | solution.py:184
  265.1 8.6 %conditional.15 = ((f32[1,45,16,64]{3,1,2,0:T(8,128)S(1)}, f32[2,5,3,45,1024]{4,0,3,2,1:T(2,128)})) conditional(s32[]{:T(128)} %convert_element_type.321, (f32[1,45,16,64]{3,1,2,0:T(8,128)S(1)}, f32[2,5,3,45,1024]{4,0,3,2,1:T(2,128)}) %tuple.267, (s32[]{:T(128)}, bf16[2,5,3,45,1024]{4,3,2,1,0:T(8,128)(2,1)}, f32[5]{0:T(128)S(1)}, ...), branch_computations={%region_22.22_spmd, %region_23.23_spmd} | conditional | flops 21285380 | bytes 6566911 | solution.py:184
  274.9 8.6 %conditional.15 = ((f32[1,45,16,64]{3,1,2,0:T(8,128)S(1)}, f32[2,5,3,45,1024]{4,0,3,2,1:T(2,128)})) conditional(s32[]{:T(128)} %convert_element_type.321, (f32[1,45,16,64]{3,1,2,0:T(8,128)S(1)}, f32[2,5,3,45,1024]{4,0,3,2,1:T(2,128)}) %tuple.267, (s32[]{:T(128)}, bf16[2,5,3,45,1024]{4,3,2,1,0:T(8,128)(2,1)}, f32[5]{0:T(128)S(1)}, ...), branch_computations={%region_22.22_spmd, %region_23.23_spmd} | conditional | flops 21285380 | bytes 6566911 | solution.py:184
  284.6 8.6 %conditional.15 = ((f32[1,45,16,64]{3,1,2,0:T(8,128)S(1)}, f32[2,5,3,45,1024]{4,0,3,2,1:T(2,128)})) conditional(s32[]{:T(128)} %convert_element_type.321, (f32[1,45,16,64]{3,1,2,0:T(8,128)S(1)}, f32[2,5,3,45,1024]{4,0,3,2,1:T(2,128)}) %tuple.267, (s32[]{:T(128)}, bf16[2,5,3,45,1024]{4,3,2,1,0:T(8,128)(2,1)}, f32[5]{0:T(128)S(1)}, ...), branch_computations={%region_22.22_spmd, %region_23.23_spmd} | conditional | flops 21285380 | bytes 6566911 | solution.py:184
  294.4 8.6 %conditional.15 = ((f32[1,45,16,64]{3,1,2,0:T(8,128)S(1)}, f32[2,5,3,45,1024]{4,0,3,2,1:T(2,128)})) conditional(s32[]{:T(128)} %convert_element_type.321, (f32[1,45,16,64]{3,1,2,0:T(8,128)S(1)}, f32[2,5,3,45,1024]{4,0,3,2,1:T(2,128)}) %tuple.267, (s32[]{:T(128)}, bf16[2,5,3,45,1024]{4,3,2,1,0:T(8,128)(2,1)}, f32[5]{0:T(128)S(1)}, ...), branch_computations={%region_22.22_spmd, %region_23.23_spmd} | conditional | flops 21285380 | bytes 6566911 | solution.py:184
  304.2 8.6 %conditional.15 = ((f32[1,45,16,64]{3,1,2,0:T(8,128)S(1)}, f32[2,5,3,45,1024]{4,0,3,2,1:T(2,128)})) conditional(s32[]{:T(128)} %convert_element_type.321, (f32[1,45,16,64]{3,1,2,0:T(8,128)S(1)}, f32[2,5,3,45,1024]{4,0,3,2,1:T(2,128)}) %tuple.267, (s32[]{:T(128)}, bf16[2,5,3,45,1024]{4,3,2,1,0:T(8,128)(2,1)}, f32[5]{0:T(128)S(1)}, ...), branch_computations={%region_22.22_spmd, %region_23.23_spmd} | conditional | flops 21285380 | bytes 6566911 | solution.py:184
  314.0 8.5 %conditional.15 = ((f32[1,45,16,64]{3,1,2,0:T(8,128)S(1)}, f32[2,5,3,45,1024]{4,0,3,2,1:T(2,128)})) conditional(s32[]{:T(128)} %convert_element_type.321, (f32[1,45,16,64]{3,1,2,0:T(8,128)S(1)}, f32[2,5,3,45,1024]{4,0,3,2,1:T(2,128)}) %tuple.267, (s32[]{:T(128)}, bf16[2,5,3,45,1024]{4,3,2,1,0:T(8,128)(2,1)}, f32[5]{0:T(128)S(1)}, ...), branch_computations={%region_22.22_spmd, %region_23.23_spmd} | conditional | flops 21285380 | bytes 6566911 | solution.py:184
  323.8 8.5 %conditional.15 = ((f32[1,45,16,64]{3,1,2,0:T(8,128)S(1)}, f32[2,5,3,45,1024]{4,0,3,2,1:T(2,128)})) conditional(s32[]{:T(128)} %convert_element_type.321, (f32[1,45,16,64]{3,1,2,0:T(8,128)S(1)}, f32[2,5,3,45,1024]{4,0,3,2,1:T(2,128)}) %tuple.267, (s32[]{:T(128)}, bf16[2,5,3,45,1024]{4,3,2,1,0:T(8,128)(2,1)}, f32[5]{0:T(128)S(1)}, ...), branch_computations={%region_22.22_spmd, %region_23.23_spmd} | conditional | flops 21285380 | bytes 6566911 | solution.py:184
  333.6 67.9 %while.106 = (s32[]{:T(128)}, f32[1,45,16,64]{3,1,2,0:T(8,128)S(1)}, f32[2,5,3,45,1024]{4,0,3,2,1:T(2,128)}, s32[3,9]{1,0:T(4,128)S(1)}, bf16[2,5,3,45,1024]{4,3...) while((s32[]{:T(128)}, f32[1,45,16,64]{3,1,2,0:T(8,128)S(1)}, ...), condition=%wide.region_28.29_spmd, body=%wide.region_25.28_spmd.sunk | while | flops 21285384 | bytes 6567162 | solution.py:186
  334.7 8.3 %conditional.16 = ((f32[1,45,16,64]{3,1,2,0:T(8,128)S(1)}, f32[2,5,3,45,1024]{4,0,3,2,1:T(2,128)})) conditional(s32[]{:T(128)} %convert_element_type.322, (f32[1,45,16,64]{3,1,2,0:T(8,128)S(1)}, f32[2,5,3,45,1024]{4,0,3,2,1:T(2,128)}) %tuple.270, (s32[]{:T(128)}, bf16[2,5,3,45,1024]{4,3,2,1,0:T(8,128)(2,1)}, f32[5]{0:T(128)S(1)}, ...), branch_computations={%region_26.26_spmd, %region_27.27_spmd} | conditional | flops 21285380 | bytes 6566923 | solution.py:184
  344.1 8.3 %conditional.16 = ((f32[1,45,16,64]{3,1,2,0:T(8,128)S(1)}, f32[2,5,3,45,1024]{4,0,3,2,1:T(2,128)})) conditional(s32[]{:T(128)} %convert_element_type.322, (f32[1,45,16,64]{3,1,2,0:T(8,128)S(1)}, f32[2,5,3,45,1024]{4,0,3,2,1:T(2,128)}) %tuple.270, (s32[]{:T(128)}, bf16[2,5,3,45,1024]{4,3,2,1,0:T(8,128)(2,1)}, f32[5]{0:T(128)S(1)}, ...), branch_computations={%region_26.26_spmd, %region_27.27_spmd} | conditional | flops 21285380 | bytes 6566923 | solution.py:184
  353.5 8.3 %conditional.16 = ((f32[1,45,16,64]{3,1,2,0:T(8,128)S(1)}, f32[2,5,3,45,1024]{4,0,3,2,1:T(2,128)})) conditional(s32[]{:T(128)} %convert_element_type.322, (f32[1,45,16,64]{3,1,2,0:T(8,128)S(1)}, f32[2,5,3,45,1024]{4,0,3,2,1:T(2,128)}) %tuple.270, (s32[]{:T(128)}, bf16[2,5,3,45,1024]{4,3,2,1,0:T(8,128)(2,1)}, f32[5]{0:T(128)S(1)}, ...), branch_computations={%region_26.26_spmd, %region_27.27_spmd} | conditional | flops 21285380 | bytes 6566923 | solution.py:184
  362.8 8.3 %conditional.16 = ((f32[1,45,16,64]{3,1,2,0:T(8,128)S(1)}, f32[2,5,3,45,1024]{4,0,3,2,1:T(2,128)})) conditional(s32[]{:T(128)} %convert_element_type.322, (f32[1,45,16,64]{3,1,2,0:T(8,128)S(1)}, f32[2,5,3,45,1024]{4,0,3,2,1:T(2,128)}) %tuple.270, (s32[]{:T(128)}, bf16[2,5,3,45,1024]{4,3,2,1,0:T(8,128)(2,1)}, f32[5]{0:T(128)S(1)}, ...), branch_computations={%region_26.26_spmd, %region_27.27_spmd} | conditional | flops 21285380 | bytes 6566923 | solution.py:184
  372.2 8.3 %conditional.16 = ((f32[1,45,16,64]{3,1,2,0:T(8,128)S(1)}, f32[2,5,3,45,1024]{4,0,3,2,1:T(2,128)})) conditional(s32[]{:T(128)} %convert_element_type.322, (f32[1,45,16,64]{3,1,2,0:T(8,128)S(1)}, f32[2,5,3,45,1024]{4,0,3,2,1:T(2,128)}) %tuple.270, (s32[]{:T(128)}, bf16[2,5,3,45,1024]{4,3,2,1,0:T(8,128)(2,1)}, f32[5]{0:T(128)S(1)}, ...), branch_computations={%region_26.26_spmd, %region_27.27_spmd} | conditional | flops 21285380 | bytes 6566923 | solution.py:184
  381.5 8.3 %conditional.16 = ((f32[1,45,16,64]{3,1,2,0:T(8,128)S(1)}, f32[2,5,3,45,1024]{4,0,3,2,1:T(2,128)})) conditional(s32[]{:T(128)} %convert_element_type.322, (f32[1,45,16,64]{3,1,2,0:T(8,128)S(1)}, f32[2,5,3,45,1024]{4,0,3,2,1:T(2,128)}) %tuple.270, (s32[]{:T(128)}, bf16[2,5,3,45,1024]{4,3,2,1,0:T(8,128)(2,1)}, f32[5]{0:T(128)S(1)}, ...), branch_computations={%region_26.26_spmd, %region_27.27_spmd} | conditional | flops 21285380 | bytes 6566923 | solution.py:184
  390.9 8.3 %conditional.16 = ((f32[1,45,16,64]{3,1,2,0:T(8,128)S(1)}, f32[2,5,3,45,1024]{4,0,3,2,1:T(2,128)})) conditional(s32[]{:T(128)} %convert_element_type.322, (f32[1,45,16,64]{3,1,2,0:T(8,128)S(1)}, f32[2,5,3,45,1024]{4,0,3,2,1:T(2,128)}) %tuple.270, (s32[]{:T(128)}, bf16[2,5,3,45,1024]{4,3,2,1,0:T(8,128)(2,1)}, f32[5]{0:T(128)S(1)}, ...), branch_computations={%region_26.26_spmd, %region_27.27_spmd} | conditional | flops 21285380 | bytes 6566923 | solution.py:184
  401.5 91.5 %while.107 = (s32[]{:T(128)}, f32[1,45,16,64]{3,1,2,0:T(8,128)S(1)}, f32[2,5,3,45,1024]{4,0,3,2,1:T(2,128)}, s32[3,9]{1,0:T(4,128)S(1)}, bf16[2,5,3,45,1024]{4,3...) while((s32[]{:T(128)}, f32[1,45,16,64]{3,1,2,0:T(8,128)S(1)}, ...), condition=%wide.region_32.33_spmd, body=%wide.region_29.32_spmd.sunk | while | flops 21285384 | bytes 6567162 | solution.py:186
  402.8 9.1 %conditional.17 = ((f32[1,45,16,64]{3,1,2,0:T(8,128)S(1)}, f32[2,5,3,45,1024]{4,0,3,2,1:T(2,128)})) conditional(s32[]{:T(128)} %convert_element_type.323, (f32[1,45,16,64]{3,1,2,0:T(8,128)S(1)}, f32[2,5,3,45,1024]{4,0,3,2,1:T(2,128)}) %tuple.273, (s32[]{:T(128)}, bf16[2,5,3,45,1024]{4,3,2,1,0:T(8,128)(2,1)}, f32[5]{0:T(128)S(1)}, ...), branch_computations={%region_30.30_spmd, %region_31.31_spmd} | conditional | flops 21285380 | bytes 6566923 | solution.py:184
  413.0 9.0 %conditional.17 = ((f32[1,45,16,64]{3,1,2,0:T(8,128)S(1)}, f32[2,5,3,45,1024]{4,0,3,2,1:T(2,128)})) conditional(s32[]{:T(128)} %convert_element_type.323, (f32[1,45,16,64]{3,1,2,0:T(8,128)S(1)}, f32[2,5,3,45,1024]{4,0,3,2,1:T(2,128)}) %tuple.273, (s32[]{:T(128)}, bf16[2,5,3,45,1024]{4,3,2,1,0:T(8,128)(2,1)}, f32[5]{0:T(128)S(1)}, ...), branch_computations={%region_30.30_spmd, %region_31.31_spmd} | conditional | flops 21285380 | bytes 6566923 | solution.py:184
  423.1 9.0 %conditional.17 = ((f32[1,45,16,64]{3,1,2,0:T(8,128)S(1)}, f32[2,5,3,45,1024]{4,0,3,2,1:T(2,128)})) conditional(s32[]{:T(128)} %convert_element_type.323, (f32[1,45,16,64]{3,1,2,0:T(8,128)S(1)}, f32[2,5,3,45,1024]{4,0,3,2,1:T(2,128)}) %tuple.273, (s32[]{:T(128)}, bf16[2,5,3,45,1024]{4,3,2,1,0:T(8,128)(2,1)}, f32[5]{0:T(128)S(1)}, ...), branch_computations={%region_30.30_spmd, %region_31.31_spmd} | conditional | flops 21285380 | bytes 6566923 | solution.py:184
  433.2 9.0 %conditional.17 = ((f32[1,45,16,64]{3,1,2,0:T(8,128)S(1)}, f32[2,5,3,45,1024]{4,0,3,2,1:T(2,128)})) conditional(s32[]{:T(128)} %convert_element_type.323, (f32[1,45,16,64]{3,1,2,0:T(8,128)S(1)}, f32[2,5,3,45,1024]{4,0,3,2,1:T(2,128)}) %tuple.273, (s32[]{:T(128)}, bf16[2,5,3,45,1024]{4,3,2,1,0:T(8,128)(2,1)}, f32[5]{0:T(128)S(1)}, ...), branch_computations={%region_30.30_spmd, %region_31.31_spmd} | conditional | flops 21285380 | bytes 6566923 | solution.py:184
  443.4 9.0 %conditional.17 = ((f32[1,45,16,64]{3,1,2,0:T(8,128)S(1)}, f32[2,5,3,45,1024]{4,0,3,2,1:T(2,128)})) conditional(s32[]{:T(128)} %convert_element_type.323, (f32[1,45,16,64]{3,1,2,0:T(8,128)S(1)}, f32[2,5,3,45,1024]{4,0,3,2,1:T(2,128)}) %tuple.273, (s32[]{:T(128)}, bf16[2,5,3,45,1024]{4,3,2,1,0:T(8,128)(2,1)}, f32[5]{0:T(128)S(1)}, ...), branch_computations={%region_30.30_spmd, %region_31.31_spmd} | conditional | flops 21285380 | bytes 6566923 | solution.py:184
  453.5 9.0 %conditional.17 = ((f32[1,45,16,64]{3,1,2,0:T(8,128)S(1)}, f32[2,5,3,45,1024]{4,0,3,2,1:T(2,128)})) conditional(s32[]{:T(128)} %convert_element_type.323, (f32[1,45,16,64]{3,1,2,0:T(8,128)S(1)}, f32[2,5,3,45,1024]{4,0,3,2,1:T(2,128)}) %tuple.273, (s32[]{:T(128)}, bf16[2,5,3,45,1024]{4,3,2,1,0:T(8,128)(2,1)}, f32[5]{0:T(128)S(1)}, ...), branch_computations={%region_30.30_spmd, %region_31.31_spmd} | conditional | flops 21285380 | bytes 6566923 | solution.py:184
  463.6 9.0 %conditional.17 = ((f32[1,45,16,64]{3,1,2,0:T(8,128)S(1)}, f32[2,5,3,45,1024]{4,0,3,2,1:T(2,128)})) conditional(s32[]{:T(128)} %convert_element_type.323, (f32[1,45,16,64]{3,1,2,0:T(8,128)S(1)}, f32[2,5,3,45,1024]{4,0,3,2,1:T(2,128)}) %tuple.273, (s32[]{:T(128)}, bf16[2,5,3,45,1024]{4,3,2,1,0:T(8,128)(2,1)}, f32[5]{0:T(128)S(1)}, ...), branch_computations={%region_30.30_spmd, %region_31.31_spmd} | conditional | flops 21285380 | bytes 6566923 | solution.py:184
  473.8 9.1 %conditional.17 = ((f32[1,45,16,64]{3,1,2,0:T(8,128)S(1)}, f32[2,5,3,45,1024]{4,0,3,2,1:T(2,128)})) conditional(s32[]{:T(128)} %convert_element_type.323, (f32[1,45,16,64]{3,1,2,0:T(8,128)S(1)}, f32[2,5,3,45,1024]{4,0,3,2,1:T(2,128)}) %tuple.273, (s32[]{:T(128)}, bf16[2,5,3,45,1024]{4,3,2,1,0:T(8,128)(2,1)}, f32[5]{0:T(128)S(1)}, ...), branch_computations={%region_30.30_spmd, %region_31.31_spmd} | conditional | flops 21285380 | bytes 6566923 | solution.py:184
  483.9 9.0 %conditional.17 = ((f32[1,45,16,64]{3,1,2,0:T(8,128)S(1)}, f32[2,5,3,45,1024]{4,0,3,2,1:T(2,128)})) conditional(s32[]{:T(128)} %convert_element_type.323, (f32[1,45,16,64]{3,1,2,0:T(8,128)S(1)}, f32[2,5,3,45,1024]{4,0,3,2,1:T(2,128)}) %tuple.273, (s32[]{:T(128)}, bf16[2,5,3,45,1024]{4,3,2,1,0:T(8,128)(2,1)}, f32[5]{0:T(128)S(1)}, ...), branch_computations={%region_30.30_spmd, %region_31.31_spmd} | conditional | flops 21285380 | bytes 6566923 | solution.py:184
  493.0 4.6 convert.12
  506.1 7.0 %collective-permute-done.4 = bf16[2,5,1,45,1024]{4,0,3,2,1:T(2,128)(2,1)S(1)} collective-permute-done((bf16[2,5,1,45,1024]{4,0,3,2,1:T(2,128)(2,1)S(1)}, bf16[2,5,1,45,1024]{4,0,3,2,1:T(2,128)(2,1)S(1)}, u32[]{:S(2)}, u32[]{:S(2)}) %collective-permute-start.4) | collective-permute-done | bytes 921632 | tf_op jit(solution)/shard_map/ppermute | solution.py:31
  513.0 16.9 %collective-permute-done.5 = bf16[2,5,1,45,1024]{4,0,3,2,1:T(2,128)(2,1)S(1)} collective-permute-done((bf16[2,5,1,45,1024]{4,0,3,2,1:T(2,128)(2,1)S(1)}, bf16[2,5,1,45,1024]{4,0,3,2,1:T(2,128)(2,1)S(1)}, u32[]{:S(2)}, u32[]{:S(2)}) %collective-permute-start.5) | collective-permute-done | bytes 921632 | tf_op jit(solution)/shard_map/ppermute | solution.py:31
  532.0 57.1 %collective-permute-start.6 = (bf16[2,1,1,45,1024]{4,3,1,2,0:T(8,128)(2,1)S(1)}, bf16[2,1,1,45,1024]{4,3,1,2,0:T(8,128)(2,1)S(1)}, u32[]{:S(2)}, u32[]{:S(2)}) collective-permute-start(bf16[2,1,1,45,1024]{4,3,1,2,0:T(8,128)(2,1)S(1)} %get-tuple-element.1588), channel_id=1, source_target_pairs={{0,32},{32,64},{64,96},{96,128},{128,160},{160,192},{192,224},{224... | collective-permute-start | bytes 552968 | tf_op jit(solution)/shard_map/ppermute | solution.py:37
  595.7 16.4 %collective-permute-done.7 = bf16[2,1,1,45,1024]{4,3,1,2,0:T(8,128)(2,1)S(1)} collective-permute-done((bf16[2,1,1,45,1024]{4,3,1,2,0:T(8,128)(2,1)S(1)}, bf16[2,1,1,45,1024]{4,3,1,2,0:T(8,128)(2,1)S(1)}, u32[]{:S(2)}, u32[]{:S(2)}) %collective-permute-start.7) | collective-permute-done | bytes 184352 | tf_op jit(solution)/shard_map/ppermute | solution.py:37
  (762 shorter events, 329.8 us)
Async XLA Ops:
  0.6 37.4 %copy-start = (s32[48,9]{0,1:T(8,128)S(1)}, s32[48,9]{0,1:T(8,128)}, u32[]{:S(2)}) copy-start(s32[48,9]{0,1:T(8,128)} %param.47) | copy-start | bytes 5188
  0.6 37.5 %copy-start.8 = (bf16[3,45,1024]{2,1,0:T(8,128)(2,1)S(1)}, bf16[3,45,1024]{2,1,0:T(8,128)(2,1)}, u32[]{:S(2)}) copy-start(bf16[3,45,1024]{2,1,0:T(8,128)(2,1)} %param.43) | copy-start | bytes 829444
  1.8 20.5 %collective-permute-start = (bf16[2,1,1,45,1024]{4,3,1,0,2:T(8,128)(2,1)S(1)}, bf16[2,1,1,45,1024]{4,3,1,0,2:T(8,128)(2,1)S(1)}, u32[]{:S(2)}, u32[]{:S(2)}) collective-permute-start(bf16[2,1,1,45,1024]{4,3,1,0,2:T(8,128)(2,1)S(1)} %get-tuple-element.1591), channel_id=1, source_target_pairs={{0,32},{32,64},{64,96},{96,128},{128,160},{160,192},{192,224},{224... | collective-permute-start | bytes 552968 | tf_op jit(solution)/shard_map/ppermute | solution.py:19
  11.3 27.4 %copy-start.7 = (bf16[3,45,1024]{2,1,0:T(8,128)(2,1)S(1)}, bf16[3,45,1024]{2,1,0:T(8,128)(2,1)}, u32[]{:S(2)}) copy-start(bf16[3,45,1024]{2,1,0:T(8,128)(2,1)} %param.46) | copy-start | bytes 829444
  11.3 19.4 %collective-permute-start.1 = (bf16[2,1,1,45,1024]{4,3,1,0,2:T(8,128)(2,1)S(1)}, bf16[2,1,1,45,1024]{4,3,1,0,2:T(8,128)(2,1)S(1)}, u32[]{:S(2)}, u32[]{:S(2)}) collective-permute-start(bf16[2,1,1,45,1024]{4,3,1,0,2:T(8,128)(2,1)S(1)} %get-tuple-element.1592), channel_id=1, source_target_pairs={{32,0},{64,32},{96,64},{128,96},{160,128},{192,160},{224,192},{256... | collective-permute-start | bytes 552968 | tf_op jit(solution)/shard_map/ppermute | solution.py:21
  30.8 8.5 %copy-start.9 = (s32[48]{0:T(128)S(1)}, s32[48]{0:T(128)}, u32[]{:S(2)}) copy-start(s32[48]{0:T(128)} %param.48) | copy-start | bytes 580
  30.8 8.6 %copy-start.10 = (f32[32]{0:T(128)S(1)}, f32[32]{0:T(128)}, u32[]{:S(2)}) copy-start(f32[32]{0:T(128)} %param.49) | copy-start | bytes 388
  32.7 24.7 %collective-permute-start.3 = (bf16[2,5,1,45,1024]{4,0,3,2,1:T(2,128)(2,1)}, bf16[2,5,1,45,1024]{4,0,3,2,1:T(2,128)(2,1)}, u32[]{:S(2)}, u32[]{:S(2)}) collective-permute-start(bf16[2,5,1,45,1024]{4,0,3,2,1:T(2,128)(2,1)} %copy.219), channel_id=1, source_target_pairs={{1,0},{2,1},{3,2},{4,3},{5,4},{6,5},{7,6},{8,7},{9,8},{10,9},{11,1... | collective-permute-start | bytes 2764808 | tf_op jit(solution)/shard_map/ppermute | solution.py:21
  34.6 40.2 %collective-permute-start.2 = (bf16[2,5,1,45,1024]{4,0,3,2,1:T(2,128)(2,1)}, bf16[2,5,1,45,1024]{4,0,3,2,1:T(2,128)(2,1)}, u32[]{:S(2)}, u32[]{:S(2)}) collective-permute-start(bf16[2,5,1,45,1024]{4,0,3,2,1:T(2,128)(2,1)} %copy.219), channel_id=1, source_target_pairs={{0,1},{1,2},{2,3},{3,4},{4,5},{5,6},{6,7},{7,8},{8,9},{9,10},{10,1... | collective-permute-start | bytes 2764808 | tf_op jit(solution)/shard_map/ppermute | solution.py:19
  129.6 118.6 %copy-start.1 = (bf16[1,45,16,64]{3,2,1,0:T(8,128)(2,1)}, bf16[1,45,16,64]{3,2,1,0:T(8,128)(2,1)S(1)}, u32[]{:S(2)}) copy-start(bf16[1,45,16,64]{3,2,1,0:T(8,128)(2,1)S(1)} %copy.228) | copy-start | bytes 276484
  191.5 56.5 %copy-start.3 = (bf16[1,45,16,64]{3,2,1,0:T(8,128)(2,1)}, bf16[1,45,16,64]{3,2,1,0:T(8,128)(2,1)S(1)}, u32[]{:S(2)}) copy-start(bf16[1,45,16,64]{3,2,1,0:T(8,128)(2,1)S(1)} %copy.231) | copy-start | bytes 276484
  247.8 2.3 copy-start.5
  493.0 11.2 %slice-start = ((s8[5529600]{0:T(1024)(128)(4,1)}), s8[4194304]{0:T(1024)(128)(4,1)S(1)}, s32[]{:S(2)}) async-start(s8[5529600]{0:T(1024)(128)(4,1)} %bitcast.246), calls=%async_computation | async-start | bytes 8388608
  493.0 11.2 %slice-start.1 = ((s8[5529600]{0:T(1024)(128)(4,1)}), s8[1335296]{0:T(1024)(128)(4,1)S(1)}, s32[]{:S(2)}) async-start(s8[5529600]{0:T(1024)(128)(4,1)} %bitcast.246), calls=%async_computation.1 | async-start | bytes 2670592
  498.9 14.2 %collective-permute-start.4 = (bf16[2,5,1,45,1024]{4,0,3,2,1:T(2,128)(2,1)S(1)}, bf16[2,5,1,45,1024]{4,0,3,2,1:T(2,128)(2,1)S(1)}, u32[]{:S(2)}, u32[]{:S(2)}) collective-permute-start(bf16[2,5,1,45,1024]{4,0,3,2,1:T(2,128)(2,1)S(1)} %get-tuple-element.1585), channel_id=1, source_target_pairs={{31,0},{0,1},{1,2},{2,3},{3,4},{4,5},{5,6},{6,7},{7,8},{8,9},{9,10... | collective-permute-start | bytes 2764808 | tf_op jit(solution)/shard_map/ppermute | solution.py:31
  502.2 27.7 %collective-permute-start.5 = (bf16[2,5,1,45,1024]{4,0,3,2,1:T(2,128)(2,1)S(1)}, bf16[2,5,1,45,1024]{4,0,3,2,1:T(2,128)(2,1)S(1)}, u32[]{:S(2)}, u32[]{:S(2)}) collective-permute-start(bf16[2,5,1,45,1024]{4,0,3,2,1:T(2,128)(2,1)S(1)} %get-tuple-element.1586), channel_id=1, source_target_pairs={{1,0},{2,1},{3,2},{4,3},{5,4},{6,5},{7,6},{8,7},{9,8},{10,9},{11,1... | collective-permute-start | bytes 2764808 | tf_op jit(solution)/shard_map/ppermute | solution.py:31
  506.0 83.1 %copy-start.6 = (bf16[1,45,16,64]{3,2,1,0:T(8,128)(2,1)S(1)}, bf16[1,45,16,64]{3,2,1,0:T(8,128)(2,1)}, u32[]{:S(2)}) copy-start(bf16[1,45,16,64]{3,2,1,0:T(8,128)(2,1)} %copy-done.5) | copy-start | bytes 276484
  506.0 83.3 %copy-start.4 = (bf16[1,45,16,64]{3,2,1,0:T(8,128)(2,1)S(1)}, bf16[1,45,16,64]{3,2,1,0:T(8,128)(2,1)}, u32[]{:S(2)}) copy-start(bf16[1,45,16,64]{3,2,1,0:T(8,128)(2,1)} %copy-done.3) | copy-start | bytes 276484
  506.0 83.4 %copy-start.2 = (bf16[1,45,16,64]{3,2,1,0:T(8,128)(2,1)S(1)}, bf16[1,45,16,64]{3,2,1,0:T(8,128)(2,1)}, u32[]{:S(2)}) copy-start(bf16[1,45,16,64]{3,2,1,0:T(8,128)(2,1)} %copy-done.1) | copy-start | bytes 276484
  532.0 62.6 %collective-permute-start.6 = (bf16[2,1,1,45,1024]{4,3,1,2,0:T(8,128)(2,1)S(1)}, bf16[2,1,1,45,1024]{4,3,1,2,0:T(8,128)(2,1)S(1)}, u32[]{:S(2)}, u32[]{:S(2)}) collective-permute-start(bf16[2,1,1,45,1024]{4,3,1,2,0:T(8,128)(2,1)S(1)} %get-tuple-element.1588), channel_id=1, source_target_pairs={{0,32},{32,64},{64,96},{96,128},{128,160},{160,192},{192,224},{224... | collective-permute-start | bytes 552968 | tf_op jit(solution)/shard_map/ppermute | solution.py:37
  591.3 20.8 %collective-permute-start.7 = (bf16[2,1,1,45,1024]{4,3,1,2,0:T(8,128)(2,1)S(1)}, bf16[2,1,1,45,1024]{4,3,1,2,0:T(8,128)(2,1)S(1)}, u32[]{:S(2)}, u32[]{:S(2)}) collective-permute-start(bf16[2,1,1,45,1024]{4,3,1,2,0:T(8,128)(2,1)S(1)} %get-tuple-element.1587), channel_id=1, source_target_pairs={{32,0},{64,32},{96,64},{128,96},{160,128},{192,160},{224,192},{256... | collective-permute-start | bytes 552968 | tf_op jit(solution)/shard_map/ppermute | solution.py:37
where the time goes:
time: 619 us; the launch traced here: 613 us
  local copies, waits for them, and re-layouts  164 us (26%)
  loops' own time  120 us (19%)
  waiting for transfers between devices  91.4 us (15%)
  other arithmetic  83 us (13%)
  starting transfers between devices  81 us (13%)
  matrix products  72.6 us (12%)
    another operation x54, loops' own time, visit_slot(): lax.cond(pair_code >= 0, take_pair, lambda state_carry: state_carry, stat...  87.6 us
    ppermute x2, starting transfers between devices, from_behind(): return lax.ppermute(value, axis, pairs)  59 us
    dynamic_update_slice x24, other arithmetic, take_pair(): lax.dynamic_update_slice(grad_buffer, previous + both_parts, corner_index)  52.2 us
    slice x48, local copies, waits for them, and re-layouts, key_block(): return (split_heads(kv_block[0, 0]), split_heads(kv_block[1, 0]), weight)  45.8 us
    dynamic_slice x54, local copies, waits for them, and re-layouts, visit_slot(): pair_code = own_codes[row_index, slot_index]  30.7 us
    dynamic_slice x48, local copies, waits for them, and re-layouts, key_block(): weight = lax.dynamic_index_in_dim(ext_weight, lat_pos, 0, keepdims=False)  29.8 us
    ppermute x2, waiting for transfers between devices, extended(): lax.ppermute(head, axis, [((i + 1) % count, i) for i in range(count)])  26.1 us
    dot_general x48, matrix products, pair_scores(): jnp.einsum('tqhd,tkhd->thqk', query_tile, key_tile, preferred_element_typ...  26 us
  transfers between devices with their start and end apart: 8, of which 7 were waited for; matrix products, arithmetic and copies ran while one was open for 2% of the time, Pallas kernels for 0%

commit v1 on v0

v1 whole, which is shorter than its diff:
```python
import jax
import jax.numpy as jnp
from jax import lax
from jax.experimental import pallas as pl
from jax.experimental.pallas import tpu as pltpu
from jax.sharding import PartitionSpec as P

HEADS = 16
HEAD = 64
TILE = 45
PAD = 48
NPAIR = 9
HALF = 512
GROUP = 256
STACK = 4 * PAD
SCALE = HEAD ** (-0.5)
MESH = pl.DeviceIdType.MESH
NT = (((1,), (1,)), ((), ()))


def dot_nt(a, b):
    return lax.dot_general(a, b, NT, preferred_element_type=jnp.float32)


def dot_nn(a, b):
    return jnp.dot(a, b, preferred_element_type=jnp.float32)


def stacked(tile):
    head = lax.broadcasted_iota(jnp.int32, (PAD, GROUP), 1) // HEAD
    return jnp.concatenate([jnp.where(head == h, tile, jnp.zeros_like(tile)) for h in range(4)], axis=0)


def unstacked(blocks):
    head = lax.broadcasted_iota(jnp.int32, (PAD, GROUP), 1) // HEAD
    out = blocks[0:PAD]
    for h in range(1, 4):
        out = jnp.where(head == h, blocks[h * PAD : (h + 1) * PAD], out)
    return out


def kernel(q_in, k_in, v_in, g_in, pair_ref, index_ref, table_ref, o_out, dq_out, dk_out, dv_out,
           stage, buf, stats, dk_acc, dv_acc, result, landed, ssem, rsem):
    lat_size, lon_size = lax.axis_size("lat"), lax.axis_size("lon")
    lat, lon = lax.axis_index("lat"), lax.axis_index("lon")
    bands = lat_size // 2
    rows = lat_size * 3
    core = lax.rem(lat, 2)
    band = lat // 2
    other = 1 - core
    east = lax.rem(lon + 1, lon_size)
    west = lax.rem(lon + lon_size - 1, lon_size)
    sides = (east, west)
    up = lax.rem(band + 1, bands)
    down = lax.rem(band + bands - 1, bands)
    toward = lax.rem(band + 2 * core - 1 + bands, bands)
    away = lax.rem(band + 1 - 2 * core + bands, bands)
    partner = (2 * band + other, lon)

    barrier = pltpu.get_barrier_semaphore()
    greeted = [partner]
    for side in sides:
        for h in range(2):
            greeted.append((2 * band + h, side))
    greeted += [(2 * toward, lon), (2 * toward + 1, lon), (2 * away + core, lon)]
    for device in greeted:
        pl.semaphore_signal(barrier, inc=1, device_id=device, device_id_type=MESH)

    mine = 1 + 3 * core

    def fill(pair, arrays):
        for a, ref in enumerate(arrays):
            for r in range(3):
                for h in range(2):
                    stage[pair, h, a, r, 32:PAD, :] = jnp.zeros((PAD - 32, HALF), jnp.bfloat16)
                    stage[pair, h, a, r, 0:TILE, :] = ref[r, :, h * HALF : (h + 1) * HALF]

    def own(pair):
        for a in range(2):
            for r in range(3):
                buf[pair, a, 1, mine + r] = stage[pair, core, a, r]

    def send(src, dst, s, r, device):
        return pltpu.make_async_remote_copy(
            src_ref=src, dst_ref=dst, send_sem=ssem.at[s], recv_sem=rsem.at[r],
            device_id=device, device_id_type=MESH)

    def arrive(dst, r):
        send(dst, dst, 0, r, partner).wait_recv()

    def partner_copy(p):
        return send(stage.at[p, other], buf.at[p, :, 1, pl.ds(mine, 3)], 11 * p, 11 * p, partner)

    def lat_copies(p):
        return [send(stage.at[p, h, :, 2 * core], buf.at[p, :, 1, 7 * other], 11 * p + 5 + h, 11 * p + 5 + core,
                     (2 * toward + h, lon)) for h in range(2)]

    def lon_copies(p):
        return [send(stage.at[p, h], buf.at[p, :, 2 * d, pl.ds(mine, 3)], 11 * p + 1 + 2 * d + h,
                     11 * p + 1 + 2 * d + core, (2 * band + h, sides[d])) for d in range(2) for h in range(2)]

    def corner_copies(p, e):
        return [send(buf.at[p, :, 1, 7 * e], buf.at[p, :, 2 * d, 7 * e], 11 * p + 7 + 2 * d + e,
                     11 * p + 7 + 2 * d + e, (lat, sides[d])) for d in range(2)]

    def partner_arrive(p):
        arrive(buf.at[p, :, 1, pl.ds(1 + 3 * other, 3)], 11 * p)

    def lat_arrive(p, e):
        arrive(buf.at[p, :, 1, 7 * e], 11 * p + 6 - e)

    def lon_arrive(p, d):
        for s in range(2):
            arrive(buf.at[p, :, 2 * d, pl.ds(1 + 3 * s, 3)], 11 * p + 1 + 2 * d + s)

    def corner_arrive(p, d, e):
        arrive(buf.at[p, :, 2 * d, 7 * e], 11 * p + 7 + 2 * d + e)

    def stats_lat(e):
        return send(stats.at[1, 6 - 5 * e], stats.at[1, 7 * e], 22 + e, 22 + e, (2 * (up, down)[e] + core, lon))

    def stats_lon(d):
        return send(stats.at[1, pl.ds(1, 6)], stats.at[2 * d, pl.ds(1, 6)], 24 + d, 24 + d, (lat, sides[d]))

    def stats_corner(d, e):
        return send(stats.at[1, 7 * e], stats.at[2 * d, 7 * e], 26 + 2 * d + e, 26 + 2 * d + e, (lat, sides[d]))

    def result_copy(i):
        return send(result.at[pl.ds(2 * i, 2), pl.ds(3 * other, 3)], landed.at[pl.ds(2 * i, 2)], 30 + i, 30 + i, partner)

    def global_row(r):
        return lax.rem(6 * band + r - 1 + rows, rows)

    def row_weight(r):
        return table_ref[index_ref[global_row(r)]]

    def listed(r, code):
        hit = pair_ref[global_row(r), 0] == code
        for s in range(1, NPAIR):
            hit = hit | (pair_ref[global_row(r), s] == code)
        return hit

    def query_side(r):
        at = lax.broadcasted_iota(jnp.int32, (1, 9 * PAD), 1)
        block = at // PAD
        a = lax.rem(block, 3)
        mask = listed(r, 3 * a + block // 3) & (lax.rem(at, PAD) < TILE)
        weight = jnp.where(a == 0, row_weight(r - 1), jnp.where(a == 1, row_weight(r), row_weight(r + 1)))
        eye = (lax.broadcasted_iota(jnp.int32, (STACK, STACK), 0)
               == lax.broadcasted_iota(jnp.int32, (STACK, STACK), 1))
        for g in range(2):
            lanes = slice(g * GROUP, (g + 1) * GROUP)
            keys = jnp.concatenate(
                [buf[0, 0, c, pl.ds(r - 1, 3), :, lanes].reshape(3 * PAD, GROUP) for c in range(3)], axis=0)
            values = jnp.concatenate(
                [buf[0, 1, c, pl.ds(r - 1, 3), :, lanes].reshape(3 * PAD, GROUP) for c in range(3)], axis=0)
            qm = stacked(buf[1, 0, 1, r, :, lanes])
            gm = stacked(buf[1, 1, 1, r, :, lanes])
            scores = jnp.where(mask, dot_nt(qm, keys) * SCALE, -1e30)
            row_max = jnp.max(scores, axis=1, keepdims=True)
            shares = weight * jnp.exp(scores - row_max)
            total = jnp.sum(shares, axis=1, keepdims=True)
            mixed = dot_nn(shares.astype(jnp.bfloat16), values) / total
            attended = unstacked(mixed).astype(jnp.bfloat16)
            attended4 = jnp.concatenate([attended] * 4, axis=0).astype(jnp.float32)
            delta = jnp.sum(gm.astype(jnp.float32) * attended4, axis=1, keepdims=True)
            lse = row_max + jnp.log(total)
            slopes = shares * (1.0 / total) * (dot_nt(gm, values) - delta)
            grad = dot_nn(slopes.astype(jnp.bfloat16), keys) * SCALE
            result[0, r - 1, :, lanes] = attended
            result[1, r - 1, :, lanes] = unstacked(grad).astype(jnp.bfloat16)
            stats[1, r, g : g + 1, 0:STACK] = jnp.sum(jnp.where(eye, lse, 0.0), axis=0, keepdims=True)
            stats[1, r, 2 + g : 3 + g, 0:STACK] = jnp.sum(jnp.where(eye, delta, 0.0), axis=0, keepdims=True)

    def key_side(c, r, first, count, a_first):
        at = lax.broadcasted_iota(jnp.int32, (count * PAD, 1), 0)
        a = a_first + at // PAD
        mask = listed(r, 3 * a + 2 - c) & (lax.rem(at, PAD) < TILE)
        weight = jnp.full((count * PAD, 1), row_weight(first), jnp.float32)
        for i in range(1, count):
            weight = jnp.where(at >= i * PAD, row_weight(first + i), weight)
        for g in range(2):
            lanes = slice(g * GROUP, (g + 1) * GROUP)
            keys = buf[0, 0, 1, pl.ds(first, count), :, lanes].reshape(count * PAD, GROUP)
            values = buf[0, 1, 1, pl.ds(first, count), :, lanes].reshape(count * PAD, GROUP)
            qm = stacked(buf[1, 0, c, r, :, lanes])
            gm = stacked(buf[1, 1, c, r, :, lanes])
            lse = stats[c, r, g : g + 1, 0:STACK]
            delta = stats[c, r, 2 + g : 3 + g, 0:STACK]
            probs = jnp.where(mask, weight * jnp.exp(dot_nt(keys, qm) * SCALE - lse), 0.0)
            slopes = probs * (dot_nt(values, gm) - delta)
            dv = dot_nn(probs.astype(jnp.bfloat16), gm)
            dk = dot_nn(slopes.astype(jnp.bfloat16), qm)
            dv_acc[pl.ds(first, count), :, lanes] += dv.reshape(count, PAD, GROUP)
            dk_acc[pl.ds(first, count), :, lanes] += dk.reshape(count, PAD, GROUP)

    def near(c, r):
        key_side(c, r, r - 1, 3, 0)

    def rim(c, e):
        key_side(c, 7 * e, 1 + 5 * e, 1, 2 - 2 * e)

    fill(0, (k_in, v_in))
    fill(1, (q_in, g_in))
    pl.semaphore_wait(barrier, len(greeted))
    sent = []

    def start(copies):
        for copy in copies:
            copy.start()
        sent.extend(copies)

    kv_lon = lon_copies(0)
    start(lat_copies(0))
    start([partner_copy(0), partner_copy(1)])
    for copy in kv_lon:
        copy.start()
    own(0)
    own(1)
    dk_acc[...] = jnp.zeros_like(dk_acc)
    dv_acc[...] = jnp.zeros_like(dv_acc)
    for e in range(2):
        lat_arrive(0, e)
        start(corner_copies(0, e))
    start(lat_copies(1))
    for copy in kv_lon:
        copy.wait_send()
    start(lon_copies(1))
    partner_arrive(0)
    partner_arrive(1)
    for d in range(2):
        lon_arrive(0, d)
        for e in range(2):
            corner_arrive(0, d, e)

    def query_step(i, carry):
        query_side(i + 1)
        return carry

    lax.fori_loop(0, 6, query_step, 0)
    start([stats_lat(0), stats_lat(1), stats_lon(0), stats_lon(1), result_copy(0)])

    def own_step(i, carry):
        near(1, i + 1)
        return carry

    lax.fori_loop(0, 6, own_step, 0)
    for e in range(2):
        arrive(stats.at[1, 7 * e], 22 + e)
        start([stats_corner(0, e), stats_corner(1, e)])
    for e in range(2):
        lat_arrive(1, e)
        start(corner_copies(1, e))

    def rim_step(e, carry):
        rim(1, e)
        return carry

    lax.fori_loop(0, 2, rim_step, 0)
    for d in range(2):
        arrive(stats.at[2 * d, pl.ds(1, 6)], 24 + d)
        lon_arrive(1, d)

    def side_step(i, carry):
        near(2 * (i // 6), 1 + lax.rem(i, 6))
        return carry

    lax.fori_loop(0, 12, side_step, 0)
    for d in range(2):
        for e in range(2):
            arrive(stats.at[2 * d, 7 * e], 26 + 2 * d + e)
            corner_arrive(1, d, e)

    def corner_step(i, carry):
        rim(2 * (i // 2), lax.rem(i, 2))
        return carry

    lax.fori_loop(0, 4, corner_step, 0)
    for r in range(6):
        result[2, r] = (dk_acc[r + 1] * SCALE).astype(jnp.bfloat16)
        result[3, r] = dv_acc[r + 1].astype(jnp.bfloat16)
    start([result_copy(1)])
    mine_lanes = pl.ds(pl.multiple_of(core * HALF, HALF), HALF)
    other_lanes = pl.ds(pl.multiple_of(other * HALF, HALF), HALF)
    outs = (o_out, dq_out, dk_out, dv_out)
    for i in range(2):
        arrive(landed.at[pl.ds(2 * i, 2)], 30 + i)
    for i, out in enumerate(outs):
        for r in range(3):
            out[r, :, mine_lanes] = result[i, 3 * core + r, 0:TILE, :]
            out[r, :, other_lanes] = landed[i, r, 0:TILE, :]
    for copy in sent:
        copy.wait_send()


def on_device(queries, keys, values, cotangent, pair_list, quad_index, quad_table):
    vmem = pl.BlockSpec(memory_space=pltpu.VMEM)
    smem = pl.BlockSpec(memory_space=pltpu.SMEM)
    return tuple(pl.pallas_call(
        kernel,
        out_shape=[jax.ShapeDtypeStruct(queries.shape, jnp.bfloat16)] * 4,
        in_specs=[vmem] * 4 + [smem] * 3,
        out_specs=[vmem] * 4,
        scratch_shapes=[
            pltpu.VMEM((2, 2, 2, 3, PAD, HALF), jnp.bfloat16),
            pltpu.VMEM((2, 2, 3, 8, PAD, HALF), jnp.bfloat16),
            pltpu.VMEM((3, 8, 8, 256), jnp.float32),
            pltpu.VMEM((8, PAD, HALF), jnp.float32),
            pltpu.VMEM((8, PAD, HALF), jnp.float32),
            pltpu.VMEM((4, 6, PAD, HALF), jnp.bfloat16),
            pltpu.VMEM((4, 3, PAD, HALF), jnp.bfloat16),
            pltpu.SemaphoreType.DMA((32,)),
            pltpu.SemaphoreType.DMA((32,)),
        ],
        compiler_params=pltpu.CompilerParams(
            collective_id=0, has_side_effects=True, vmem_limit_bytes=48 * 2**20),
        name="sphere",
    )(queries, keys, values, cotangent, pair_list, quad_index, quad_table))


def solution(mesh):
    grid = P("lat", "lon", None)
    return jax.shard_map(
        on_device, mesh=mesh, in_specs=(grid,) * 4 + (P(),) * 3, out_specs=(grid,) * 4, check_vma=False)
```

time: 619 us -> 145 us (0.23)
  the two profiles are of different devices: /device:TPU:223 before, /device:TPU:1 now
where the time goes in v1:
time: 145 us; the launch traced here: 144 us
  Pallas kernels  136 us (94%)
  local copies, waits for them, and re-layouts  7.5 us (5%)
    pallas_call x1, Pallas kernels, on_device(): pl.pallas_call(kernel, out_shape=[jax.ShapeDtypeStruct(queries.shape, jnp...  136 us
    unnamed x17, local copies, waits for them, and re-layouts  7.5 us

profile of v1, /device:TPU:1, one launch (start us, length us, event | category | flops | bytes accessed | tf_op | source)
XLA Modules:
  0.0 144.5 jit_solution(11934577539771139326)
XLA Ops:
  0.6 0.0 copy-start.5
  0.6 0.0 copy-start.4
  0.7 0.8 copy.11.pair_ref
  1.4 0.0 copy-done.5
  1.4 0.0 copy-done.4
  1.4 0.0 copy-start
  1.5 1.0 copy-done
  2.4 0.0 copy-start.1
  2.4 1.0 copy-done.1
  3.4 0.0 copy-start.2
  3.4 1.0 copy-done.2
  4.3 0.0 copy-start.3
  4.3 1.0 copy-done.3
  5.3 136.3 %sphere.1 = (bf16[3,45,1024]{2,1,0:T(8,128)(2,1)S(1)}, bf16[3,45,1024]{2,1,0:T(8,128)(2,1)S(1)}, bf16[3,45,1024]{2,1,0:T(8,128)(2,1)S(1)}, bf16[3,45,1024]{2,1,0:T(8,128)(2,1)S(1)}) custom-call(bf16[3,45,1024]{2,1,0:T(8,128)(2,1)S(1)} %copy-done, bf16[3,45,1024]{2,1,0:T(8,128)(2,1)S(1)} %copy-done.1, bf16[3,45,1024]{2,1,0:T(8,128)(2,1)S(1)} %copy-done.2, ...), custom_call_target="tpu_custom_call" | custom-call | tf_op jit(solution)/shard_map/sphere/pallas_call | solution.py:299
  141.6 0.7 copy.16
  142.3 0.7 copy.17
  143.1 0.7 copy.18
  143.8 0.7 copy.19
Async XLA Ops:
  0.6 0.8 copy-start.5
  0.6 0.8 copy-start.4
  1.4 1.0 copy-start
  2.4 1.0 copy-start.1
  3.4 1.0 copy-start.2
  4.3 1.0 copy-start.3

commit v2 on v1

--- a/solution.py
+++ b/solution.py
@@ -10,6 +10,8 @@
 TILE = 45
 PAD = 48
 NPAIR = 9
+RUN = 8
+VMEM_BYTES = 64 * 2**20 - 2**17
 HALF = 512
 GROUP = 256
 STACK = 4 * PAD
@@ -39,8 +41,9 @@
     return out
 
 
-def kernel(q_in, k_in, v_in, g_in, pair_ref, index_ref, table_ref, o_out, dq_out, dk_out, dv_out,
-           stage, buf, stats, dk_acc, dv_acc, result, landed, ssem, rsem):
+def kernel(q_in, k_in, v_in, g_in, pair_in, index_in, table_in, o_out, dq_out, dk_out, dv_out,
+           made, loaded, stage, buf, stats, dk_acc, dv_acc, result, landed, pair_ref, index_ref, table_ref,
+           lsem, ssem, rsem, row_ssem, row_rsem):
     lat_size, lon_size = lax.axis_size("lat"), lax.axis_size("lon")
     lat, lon = lax.axis_index("lat"), lax.axis_index("lon")
     bands = lat_size // 2
@@ -54,26 +57,32 @@
     up = lax.rem(band + 1, bands)
     down = lax.rem(band + bands - 1, bands)
     toward = lax.rem(band + 2 * core - 1 + bands, bands)
-    away = lax.rem(band + 1 - 2 * core + bands, bands)
+    place = lax.rem(lon, RUN)
     partner = (2 * band + other, lon)
 
     barrier = pltpu.get_barrier_semaphore()
     greeted = [partner]
-    for side in sides:
-        for h in range(2):
-            greeted.append((2 * band + h, side))
-    greeted += [(2 * toward, lon), (2 * toward + 1, lon), (2 * away + core, lon)]
+    greeted += [(2 * band + h, side) for side in sides for h in range(2)]
+    greeted += [(2 * b + h, to) for b in (up, down) for to in (west, lon, east) for h in range(2)]
     for device in greeted:
         pl.semaphore_signal(barrier, inc=1, device_id=device, device_id_type=MESH)
 
+    inputs = (k_in, v_in, q_in, g_in)
+    loads = [pltpu.make_async_copy(ref, loaded.at[i], lsem.at[i]) for i, ref in enumerate(inputs)]
+    small = [pltpu.make_async_copy(src, dst, lsem.at[4 + i]) for i, (src, dst) in enumerate(
+        ((pair_in, pair_ref), (index_in, index_ref), (table_in, table_ref)))]
+    for load in loads + small:
+        load.start()
+
     mine = 1 + 3 * core
 
-    def fill(pair, arrays):
-        for a, ref in enumerate(arrays):
+    def fill(pair):
+        for a in range(2):
+            loads[2 * pair + a].wait()
             for r in range(3):
                 for h in range(2):
                     stage[pair, h, a, r, 32:PAD, :] = jnp.zeros((PAD - 32, HALF), jnp.bfloat16)
-                    stage[pair, h, a, r, 0:TILE, :] = ref[r, :, h * HALF : (h + 1) * HALF]
+                    stage[pair, h, a, r, 0:TILE, :] = loaded[2 * pair + a, r, :, h * HALF : (h + 1) * HALF]
 
     def own(pair):
         for a in range(2):
@@ -89,44 +98,109 @@
         send(dst, dst, 0, r, partner).wait_recv()
 
     def partner_copy(p):
-        return send(stage.at[p, other], buf.at[p, :, 1, pl.ds(mine, 3)], 11 * p, 11 * p, partner)
-
-    def lat_copies(p):
-        return [send(stage.at[p, h, :, 2 * core], buf.at[p, :, 1, 7 * other], 11 * p + 5 + h, 11 * p + 5 + core,
-                     (2 * toward + h, lon)) for h in range(2)]
+        return send(stage.at[p, other], buf.at[p, :, 1, pl.ds(mine, 3)], 15 * p, 11 * p, partner)
 
     def lon_copies(p):
-        return [send(stage.at[p, h], buf.at[p, :, 2 * d, pl.ds(mine, 3)], 11 * p + 1 + 2 * d + h,
+        return [send(stage.at[p, h], buf.at[p, :, 2 * d, pl.ds(mine, 3)], 15 * p + 1 + 2 * d + h,
                      11 * p + 1 + 2 * d + core, (2 * band + h, sides[d])) for d in range(2) for h in range(2)]
 
-    def corner_copies(p, e):
-        return [send(buf.at[p, :, 1, 7 * e], buf.at[p, :, 2 * d, 7 * e], 11 * p + 7 + 2 * d + e,
-                     11 * p + 7 + 2 * d + e, (lat, sides[d])) for d in range(2)]
+    def lon_rows():
+        return [pltpu.make_async_remote_copy(
+            src_ref=stage.at[1, h, :, r], dst_ref=buf.at[1, :, 2 * d, mine + r],
+            send_sem=row_ssem.at[4 * r + 2 * d + h], recv_sem=row_rsem.at[4 * r + 2 * d + core],
+            device_id=(2 * band + h, sides[d]), device_id_type=MESH)
+            for r in range(3) for d in range(2) for h in range(2)]
+
+    def slot(p, col, e):
+        return buf.at[p, :, col, 7 * e]
+
+    def seam_copies(p, number, col, to):
+        return [send(stage.at[p, h, :, 2 * core], slot(p, col, other), 15 * p + number + h,
+                     11 * p + 5 + 2 * col + other, (2 * toward + h, to)) for h in range(2)]
+
+    def seam_near(p):
+        return seam_copies(p, 5, 2 * core, core * west + other * east)
+
+    def seam_same(p):
+        return seam_copies(p, 7, 1, lon)
+
+    def seam_far(p):
+        return seam_copies(p, 9, 2 * other, core * east + other * west)
+
+    def relay(p, e, step):
+        col = (2 - step, step)[e]
+        to = (1 - step, 1 + step)[e]
+        return send(slot(p, col, e), slot(p, to, e), 15 * p + 11 + 2 * step + e, 11 * p + 5 + 2 * to + e,
+                    (lat, sides[e]))
+
+    same_when = place == (RUN - 1) * other
+    far_when = place == (RUN - 1) * core
+    relay_when = (place != RUN - 1, place != 0)
+
+    def seam_start(p):
+        for copy in seam_near(p):
+            copy.start()
+
+        @pl.when(same_when)
+        def _():
+            for copy in seam_same(p):
+                copy.start()
+
+        @pl.when(far_when)
+        def _():
+            for copy in seam_far(p):
+                copy.start()
+
+    def seam_sent(p):
+        for copy in seam_near(p):
+            copy.wait_send()
+
+        @pl.when(same_when)
+        def _():
+            for copy in seam_same(p):
+                copy.wait_send()
+
+        @pl.when(far_when)
+        def _():
+            for copy in seam_far(p):
+                copy.wait_send()
+
+    def relay_start(p, step):
+        for e in range(2):
+            slot_arrive(p, ((2, 0), (1, 1))[step][e], e)
+
+            @pl.when(relay_when[e])
+            def _():
+                relay(p, e, step).start()
+
+    def relay_sent(p, step):
+        for e in range(2):
+
+            @pl.when(relay_when[e])
+            def _():
+                relay(p, e, step).wait_send()
+
+    def slot_arrive(p, col, e):
+        arrive(slot(p, col, e), 11 * p + 5 + 2 * col + e)
 
     def partner_arrive(p):
         arrive(buf.at[p, :, 1, pl.ds(1 + 3 * other, 3)], 11 * p)
-
-    def lat_arrive(p, e):
-        arrive(buf.at[p, :, 1, 7 * e], 11 * p + 6 - e)
 
     def lon_arrive(p, d):
         for s in range(2):
             arrive(buf.at[p, :, 2 * d, pl.ds(1 + 3 * s, 3)], 11 * p + 1 + 2 * d + s)
 
-    def corner_arrive(p, d, e):
-        arrive(buf.at[p, :, 2 * d, 7 * e], 11 * p + 7 + 2 * d + e)
-
     def stats_lat(e):
-        return send(stats.at[1, 6 - 5 * e], stats.at[1, 7 * e], 22 + e, 22 + e, (2 * (up, down)[e] + core, lon))
+        return send(stats.at[1, 6 - 5 * e], stats.at[1, 7 * e], 30 + e, 22 + e, (2 * (up, down)[e] + core, lon))
 
     def stats_lon(d):
-        return send(stats.at[1, pl.ds(1, 6)], stats.at[2 * d, pl.ds(1, 6)], 24 + d, 24 + d, (lat, sides[d]))
+        return send(stats.at[1, pl.ds(1, 6)], stats.at[2 * d, pl.ds(1, 6)], 32 + d, 24 + d, (lat, sides[d]))
 
     def stats_corner(d, e):
-        return send(stats.at[1, 7 * e], stats.at[2 * d, 7 * e], 26 + 2 * d + e, 26 + 2 * d + e, (lat, sides[d]))
+        return send(stats.at[1, 7 * e], stats.at[2 * d, 7 * e], 34 + 2 * d + e, 26 + 2 * d + e, (lat, sides[d]))
 
     def result_copy(i):
-        return send(result.at[pl.ds(2 * i, 2), pl.ds(3 * other, 3)], landed.at[pl.ds(2 * i, 2)], 30 + i, 30 + i, partner)
+        return send(result.at[pl.ds(2 * i, 2), pl.ds(3 * other, 3)], landed.at[pl.ds(2 * i, 2)], 38 + i, 30 + i, partner)
 
     def global_row(r):
         return lax.rem(6 * band + r - 1 + rows, rows)
@@ -135,9 +209,9 @@
         return table_ref[index_ref[global_row(r)]]
 
     def listed(r, code):
-        hit = pair_ref[global_row(r), 0] == code
+        hit = pair_ref[0, global_row(r)] == code
         for s in range(1, NPAIR):
-            hit = hit | (pair_ref[global_row(r), s] == code)
+            hit = hit | (pair_ref[s, global_row(r)] == code)
         return hit
 
     def query_side(r):
@@ -200,9 +274,6 @@
     def rim(c, e):
         key_side(c, 7 * e, 1 + 5 * e, 1, 2 - 2 * e)
 
-    fill(0, (k_in, v_in))
-    fill(1, (q_in, g_in))
-    pl.semaphore_wait(barrier, len(greeted))
     sent = []
 
     def start(copies):
@@ -210,28 +281,35 @@
             copy.start()
         sent.extend(copies)
 
-    kv_lon = lon_copies(0)
-    start(lat_copies(0))
-    start([partner_copy(0), partner_copy(1)])
-    for copy in kv_lon:
+    fill(0)
+    pl.semaphore_wait(barrier, len(greeted))
+    seam_start(0)
+    for copy in lon_copies(0):
         copy.start()
+    start([partner_copy(0)])
+    fill(1)
+    start([partner_copy(1)])
     own(0)
     own(1)
     dk_acc[...] = jnp.zeros_like(dk_acc)
     dv_acc[...] = jnp.zeros_like(dv_acc)
-    for e in range(2):
-        lat_arrive(0, e)
-        start(corner_copies(0, e))
-    start(lat_copies(1))
-    for copy in kv_lon:
-        copy.wait_send()
-    start(lon_copies(1))
+    for load in small:
+        load.wait()
+    relay_start(0, 0)
+    seam_start(1)
     partner_arrive(0)
     partner_arrive(1)
+    for copy in lon_copies(0):
+        copy.wait_send()
+    for copy in lon_rows():
+        copy.start()
+    relay_start(0, 1)
     for d in range(2):
         lon_arrive(0, d)
-        for e in range(2):
-            corner_arrive(0, d, e)
+    slot_arrive(0, 0, 0)
+    slot_arrive(0, 2, 1)
+
+    relay_start(1, 0)
 
     def query_step(i, carry):
         query_side(i + 1)
@@ -248,28 +326,46 @@
     for e in range(2):
         arrive(stats.at[1, 7 * e], 22 + e)
         start([stats_corner(0, e), stats_corner(1, e)])
-    for e in range(2):
-        lat_arrive(1, e)
-        start(corner_copies(1, e))
+    relay_start(1, 1)
 
     def rim_step(e, carry):
         rim(1, e)
         return carry
 
     lax.fori_loop(0, 2, rim_step, 0)
+    mine_lanes = pl.ds(pl.multiple_of(core * HALF, HALF), HALF)
+    other_lanes = pl.ds(pl.multiple_of(other * HALF, HALF), HALF)
+    stores = [pltpu.make_async_copy(made.at[n], out, lsem.at[7 + n])
+              for n, out in enumerate((o_out, dq_out, dk_out, dv_out))]
+
+    def write(i):
+        arrive(landed.at[pl.ds(2 * i, 2)], 30 + i)
+        for n in (2 * i, 2 * i + 1):
+            for r in range(3):
+                made[n, r, :, mine_lanes] = result[n, 3 * core + r, 0:TILE, :]
+                made[n, r, :, other_lanes] = landed[n, r, 0:TILE, :]
+            stores[n].start()
+
+    write(0)
     for d in range(2):
         arrive(stats.at[2 * d, pl.ds(1, 6)], 24 + d)
-        lon_arrive(1, d)
 
     def side_step(i, carry):
-        near(2 * (i // 6), 1 + lax.rem(i, 6))
+        r, d, s = i // 4, lax.rem(i // 2, 2), lax.rem(i, 2)
+        row = 1 + 3 * s + r
+        dst = buf.at[1, :, 2 * d, row]
+        pltpu.make_async_remote_copy(
+            src_ref=dst, dst_ref=dst, send_sem=row_ssem.at[0], recv_sem=row_rsem.at[i],
+            device_id=partner, device_id_type=MESH).wait_recv()
+        near(2 * d, row)
         return carry
 
     lax.fori_loop(0, 12, side_step, 0)
     for d in range(2):
         for e in range(2):
             arrive(stats.at[2 * d, 7 * e], 26 + 2 * d + e)
-            corner_arrive(1, d, e)
+    slot_arrive(1, 0, 0)
+    slot_arrive(1, 2, 1)
 
     def corner_step(i, carry):
         rim(2 * (i // 2), lax.rem(i, 2))
@@ -280,28 +376,35 @@
         result[2, r] = (dk_acc[r + 1] * SCALE).astype(jnp.bfloat16)
         result[3, r] = dv_acc[r + 1].astype(jnp.bfloat16)
     start([result_copy(1)])
-    mine_lanes = pl.ds(pl.multiple_of(core * HALF, HALF), HALF)
-    other_lanes = pl.ds(pl.multiple_of(other * HALF, HALF), HALF)
-    outs = (o_out, dq_out, dk_out, dv_out)
-    for i in range(2):
-        arrive(landed.at[pl.ds(2 * i, 2)], 30 + i)
-    for i, out in enumerate(outs):
-        for r in range(3):
-            out[r, :, mine_lanes] = result[i, 3 * core + r, 0:TILE, :]
-            out[r, :, other_lanes] = landed[i, r, 0:TILE, :]
-    for copy in sent:
+    write(1)
+    for copy in sent + lon_rows():
         copy.wait_send()
+    for p in range(2):
+        seam_sent(p)
+        for step in range(2):
+            relay_sent(p, step)
+    for store in stores:
+        store.wait()
+
+
+def finish(*refs):
+    for i in range(4):
+        refs[4 + i][...] = refs[i][...]
 
 
 def on_device(queries, keys, values, cotangent, pair_list, quad_index, quad_table):
     vmem = pl.BlockSpec(memory_space=pltpu.VMEM)
-    smem = pl.BlockSpec(memory_space=pltpu.SMEM)
-    return tuple(pl.pallas_call(
+    hbm = pl.BlockSpec(memory_space=pltpu.HBM)
+    pairs = pair_list.T
+    outs = [jax.ShapeDtypeStruct(queries.shape, jnp.bfloat16)] * 4
+    results = pl.pallas_call(
         kernel,
-        out_shape=[jax.ShapeDtypeStruct(queries.shape, jnp.bfloat16)] * 4,
-        in_specs=[vmem] * 4 + [smem] * 3,
-        out_specs=[vmem] * 4,
+        out_shape=outs,
+        in_specs=[hbm] * 7,
+        out_specs=[hbm] * 4,
         scratch_shapes=[
+            pltpu.VMEM((4,) + queries.shape, jnp.bfloat16),
+            pltpu.VMEM((4,) + queries.shape, jnp.bfloat16),
             pltpu.VMEM((2, 2, 2, 3, PAD, HALF), jnp.bfloat16),
             pltpu.VMEM((2, 2, 3, 8, PAD, HALF), jnp.bfloat16),
             pltpu.VMEM((3, 8, 8, 256), jnp.float32),
@@ -309,13 +412,27 @@
             pltpu.VMEM((8, PAD, HALF), jnp.float32),
             pltpu.VMEM((4, 6, PAD, HALF), jnp.bfloat16),
             pltpu.VMEM((4, 3, PAD, HALF), jnp.bfloat16),
+            pltpu.SMEM(pairs.shape, jnp.int32),
+            pltpu.SMEM(quad_index.shape, jnp.int32),
+            pltpu.SMEM(quad_table.shape, jnp.float32),
+            pltpu.SemaphoreType.DMA((11,)),
+            pltpu.SemaphoreType.DMA((40,)),
             pltpu.SemaphoreType.DMA((32,)),
-            pltpu.SemaphoreType.DMA((32,)),
+            pltpu.SemaphoreType.DMA((12,)),
+            pltpu.SemaphoreType.DMA((12,)),
         ],
         compiler_params=pltpu.CompilerParams(
-            collective_id=0, has_side_effects=True, vmem_limit_bytes=48 * 2**20),
+            collective_id=0, has_side_effects=True, vmem_limit_bytes=VMEM_BYTES),
         name="sphere",
-    )(queries, keys, values, cotangent, pair_list, quad_index, quad_table))
+    )(queries, keys, values, cotangent, pairs, quad_index, quad_table)
+    return tuple(pl.pallas_call(
+        finish,
+        out_shape=outs,
+        in_specs=[vmem] * 4,
+        out_specs=[vmem] * 4,
+        compiler_params=pltpu.CompilerParams(vmem_limit_bytes=VMEM_BYTES),
+        name="finish",
+    )(*results))
 
 
 def solution(mesh):

time: 145 us -> 135 us (0.931)
  local copies, waits for them, and re-layouts: 7.5 us -> 0 us
  Pallas kernels: 136 us -> 134 us
    unnamed x17 -> x0, local copies, waits for them, and re-layouts: 7.5 us -> none
    pallas_call x1 -> x2, Pallas kernels: 136 us -> 134 us  [the longest x1 132 us: on_device(): pl.pallas_call(kernel, out_shape=outs, in_specs=[hbm] * 7, out_specs=[hbm...]
where the time goes in v2:
time: 135 us
  Pallas kernels  134 us (99%)
    pallas_call x1, Pallas kernels, on_device(): pl.pallas_call(kernel, out_shape=outs, in_specs=[hbm] * 7, out_specs=[hbm...  132 us

profile of v2, /device:TPU:1, one launch (start us, length us, event | category | flops | bytes accessed | tf_op | source)
XLA Modules:
  0.0 134.8 jit_solution(7205706635036251782)
XLA Ops:
  0.6 131.9 %sphere.1 = (bf16[3,45,1024]{2,1,0:T(8,128)(2,1)}, bf16[3,45,1024]{2,1,0:T(8,128)(2,1)}, bf16[3,45,1024]{2,1,0:T(8,128)(2,1)}, bf16[3,45,1024]{2,1,0:T(8,128)(2,1)}) custom-call(bf16[3,45,1024]{2,1,0:T(8,128)(2,1)} %q_in.1, bf16[3,45,1024]{2,1,0:T(8,128)(2,1)} %k_in.1, bf16[3,45,1024]{2,1,0:T(8,128)(2,1)} %v_in.1, bf16[3,45,1024]{2,1,0:T(8,128)(2,1)} %g_in.1, ...), custom_call_target="tpu_custom_call" | custom-call | tf_op jit(solution)/shard_map/sphere/pallas_call | solution.py:400
  132.6 2.3 %finish.1 = (bf16[3,45,1024]{2,1,0:T(8,128)(2,1)}, bf16[3,45,1024]{2,1,0:T(8,128)(2,1)}, bf16[3,45,1024]{2,1,0:T(8,128)(2,1)}, bf16[3,45,1024]{2,1,0:T(8,128)(2,1)}) custom-call(bf16[3,45,1024]{2,1,0:T(8,128)(2,1)} %get-tuple-element.8.refs_0_, bf16[3,45,1024]{2,1,0:T(8,128)(2,1)} %get-tuple-element.9.refs_1_, ...), custom_call_target="tpu_custom_call" | custom-call | tf_op jit(solution)/shard_map/finish/pallas_call | solution.py:428

commit v3 on v2

--- a/solution.py
+++ b/solution.py
@@ -301,9 +301,9 @@
     partner_arrive(1)
     for copy in lon_copies(0):
         copy.wait_send()
-    for copy in lon_rows():
+    relay_start(0, 1)
+    for copy in lon_rows()[:8]:
         copy.start()
-    relay_start(0, 1)
     for d in range(2):
         lon_arrive(0, d)
     slot_arrive(0, 0, 0)
@@ -317,6 +317,10 @@
 
     lax.fori_loop(0, 6, query_step, 0)
     start([stats_lat(0), stats_lat(1), stats_lon(0), stats_lon(1), result_copy(0)])
+    for copy in lon_rows()[:4]:
+        copy.wait_send()
+    for copy in lon_rows()[8:]:
+        copy.start()
 
     def own_step(i, carry):
         near(1, i + 1)
@@ -377,7 +381,7 @@
         result[3, r] = dv_acc[r + 1].astype(jnp.bfloat16)
     start([result_copy(1)])
     write(1)
-    for copy in sent + lon_rows():
+    for copy in sent + lon_rows()[4:]:
         copy.wait_send()
     for p in range(2):
         seam_sent(p)

time: 135 us -> 123 us (0.911)
  Pallas kernels: 134 us -> 122 us
    pallas_call x1, Pallas kernels: 132 us -> 120 us  [on_device(): pl.pallas_call(kernel, out_shape=outs, in_specs=[hbm] * 7, out_specs=[hbm...]
where the time goes in v3:
time: 123 us
  Pallas kernels  122 us (99%)
    pallas_call x1, Pallas kernels, on_device(): pl.pallas_call(kernel, out_shape=outs, in_specs=[hbm] * 7, out_specs=[hbm...  120 us

profile of v3, /device:TPU:1, one launch (start us, length us, event | category | flops | bytes accessed | tf_op | source)
XLA Modules:
  0.0 123.0 jit_solution(8427033412788567729)
XLA Ops:
  0.6 120.1 %sphere.1 = (bf16[3,45,1024]{2,1,0:T(8,128)(2,1)}, bf16[3,45,1024]{2,1,0:T(8,128)(2,1)}, bf16[3,45,1024]{2,1,0:T(8,128)(2,1)}, bf16[3,45,1024]{2,1,0:T(8,128)(2,1)}) custom-call(bf16[3,45,1024]{2,1,0:T(8,128)(2,1)} %q_in.1, bf16[3,45,1024]{2,1,0:T(8,128)(2,1)} %k_in.1, bf16[3,45,1024]{2,1,0:T(8,128)(2,1)} %v_in.1, bf16[3,45,1024]{2,1,0:T(8,128)(2,1)} %g_in.1, ...), custom_call_target="tpu_custom_call" | custom-call | tf_op jit(solution)/shard_map/sphere/pallas_call | solution.py:404
  120.7 2.3 %finish.1 = (bf16[3,45,1024]{2,1,0:T(8,128)(2,1)}, bf16[3,45,1024]{2,1,0:T(8,128)(2,1)}, bf16[3,45,1024]{2,1,0:T(8,128)(2,1)}, bf16[3,45,1024]{2,1,0:T(8,128)(2,1)}) custom-call(bf16[3,45,1024]{2,1,0:T(8,128)(2,1)} %get-tuple-element.8.refs_0_, bf16[3,45,1024]{2,1,0:T(8,128)(2,1)} %get-tuple-element.9.refs_1_, ...), custom_call_target="tpu_custom_call" | custom-call | tf_op jit(solution)/shard_map/finish/pallas_call | solution.py:432

commit v4 on v3

--- a/solution.py
+++ b/solution.py
@@ -135,6 +135,7 @@
 
     same_when = place == (RUN - 1) * other
     far_when = place == (RUN - 1) * core
+    at_end = (place == RUN - 1, place == 0)
     relay_when = (place != RUN - 1, place != 0)
 
     def seam_start(p):
@@ -302,8 +303,14 @@
     for copy in lon_copies(0):
         copy.wait_send()
     relay_start(0, 1)
-    for copy in lon_rows()[:8]:
+    for copy in lon_rows()[:4]:
         copy.start()
+    for d in range(2):
+
+        @pl.when(at_end[d])
+        def _():
+            for copy in lon_rows()[4 + 2 * d : 6 + 2 * d] + lon_rows()[8 + 2 * d : 10 + 2 * d]:
+                copy.start()
     for d in range(2):
         lon_arrive(0, d)
     slot_arrive(0, 0, 0)
@@ -319,8 +326,12 @@
     start([stats_lat(0), stats_lat(1), stats_lon(0), stats_lon(1), result_copy(0)])
     for copy in lon_rows()[:4]:
         copy.wait_send()
-    for copy in lon_rows()[8:]:
-        copy.start()
+    for d in range(2):
+
+        @pl.when(jnp.logical_not(at_end[d]))
+        def _():
+            for copy in lon_rows()[4 + 2 * d : 6 + 2 * d] + lon_rows()[8 + 2 * d : 10 + 2 * d]:
+                copy.start()
 
     def own_step(i, carry):
         near(1, i + 1)
@@ -392,12 +403,19 @@
 
 
 def finish(*refs):
-    for i in range(4):
-        refs[4 + i][...] = refs[i][...]
+    sources, outs, held, sem = refs[:4], refs[4:8], refs[8], refs[9]
+    reads = [pltpu.make_async_copy(sources[i], held.at[i], sem.at[0, i]) for i in range(4)]
+    writes = [pltpu.make_async_copy(held.at[i], outs[i], sem.at[1, i]) for i in range(4)]
+    for read in reads:
+        read.start()
+    for read, write in zip(reads, writes):
+        read.wait()
+        write.start()
+    for write in writes:
+        write.wait()
 
 
 def on_device(queries, keys, values, cotangent, pair_list, quad_index, quad_table):
-    vmem = pl.BlockSpec(memory_space=pltpu.VMEM)
     hbm = pl.BlockSpec(memory_space=pltpu.HBM)
     pairs = pair_list.T
     outs = [jax.ShapeDtypeStruct(queries.shape, jnp.bfloat16)] * 4
@@ -432,8 +450,9 @@
     return tuple(pl.pallas_call(
         finish,
         out_shape=outs,
-        in_specs=[vmem] * 4,
-        out_specs=[vmem] * 4,
+        in_specs=[hbm] * 4,
+        out_specs=[hbm] * 4,
+        scratch_shapes=[pltpu.VMEM((4,) + queries.shape, jnp.bfloat16), pltpu.SemaphoreType.DMA((2, 4))],
         compiler_params=pltpu.CompilerParams(vmem_limit_bytes=VMEM_BYTES),
         name="finish",
     )(*results))

time: 123 us -> 123 us (level)
  no operation moved by 1% of the time
where the time goes in v4:
time: 123 us
  Pallas kernels  122 us (99%)
    pallas_call x1, Pallas kernels, on_device(): pl.pallas_call(kernel, out_shape=outs, in_specs=[hbm] * 7, out_specs=[hbm...  120 us

profile of v4, /device:TPU:1, one launch (start us, length us, event | category | flops | bytes accessed | tf_op | source)
XLA Modules:
  0.0 122.8 jit_solution(15065987244598792444)
XLA Ops:
  0.6 120.1 %sphere.1 = (bf16[3,45,1024]{2,1,0:T(8,128)(2,1)}, bf16[3,45,1024]{2,1,0:T(8,128)(2,1)}, bf16[3,45,1024]{2,1,0:T(8,128)(2,1)}, bf16[3,45,1024]{2,1,0:T(8,128)(2,1)}) custom-call(bf16[3,45,1024]{2,1,0:T(8,128)(2,1)} %q_in.1, bf16[3,45,1024]{2,1,0:T(8,128)(2,1)} %k_in.1, bf16[3,45,1024]{2,1,0:T(8,128)(2,1)} %v_in.1, bf16[3,45,1024]{2,1,0:T(8,128)(2,1)} %g_in.1, ...), custom_call_target="tpu_custom_call" | custom-call | tf_op jit(solution)/shard_map/sphere/pallas_call | solution.py:422
  120.8 2.0 %finish.1 = (bf16[3,45,1024]{2,1,0:T(8,128)(2,1)}, bf16[3,45,1024]{2,1,0:T(8,128)(2,1)}, bf16[3,45,1024]{2,1,0:T(8,128)(2,1)}, bf16[3,45,1024]{2,1,0:T(8,128)(2,1)}) custom-call(bf16[3,45,1024]{2,1,0:T(8,128)(2,1)} %get-tuple-element.8.refs_0_, bf16[3,45,1024]{2,1,0:T(8,128)(2,1)} %get-tuple-element.9.refs_1_, ...), custom_call_target="tpu_custom_call" | custom-call | tf_op jit(solution)/shard_map/finish/pallas_call | solution.py:450

commit v5 on v4

--- a/solution.py
+++ b/solution.py
@@ -285,8 +285,13 @@
     fill(0)
     pl.semaphore_wait(barrier, len(greeted))
     seam_start(0)
-    for copy in lon_copies(0):
-        copy.start()
+    for d in range(2):
+
+        @pl.when(at_end[d])
+        def _():
+            for copy in lon_copies(0)[2 * d : 2 * d + 2]:
+                copy.start()
+
     start([partner_copy(0)])
     fill(1)
     start([partner_copy(1)])
@@ -296,6 +301,13 @@
     dv_acc[...] = jnp.zeros_like(dv_acc)
     for load in small:
         load.wait()
+    for d in range(2):
+
+        @pl.when(jnp.logical_not(at_end[d]))
+        def _():
+            for copy in lon_copies(0)[2 * d : 2 * d + 2]:
+                copy.start()
+
     relay_start(0, 0)
     seam_start(1)
     partner_arrive(0)
@@ -354,10 +366,12 @@
               for n, out in enumerate((o_out, dq_out, dk_out, dv_out))]
 
     def write(i):
+        for n in (2 * i, 2 * i + 1):
+            for r in range(3):
+                made[n, r, :, mine_lanes] = result[n, 3 * core + r, 0:TILE, :]
         arrive(landed.at[pl.ds(2 * i, 2)], 30 + i)
         for n in (2 * i, 2 * i + 1):
             for r in range(3):
-                made[n, r, :, mine_lanes] = result[n, 3 * core + r, 0:TILE, :]
                 made[n, r, :, other_lanes] = landed[n, r, 0:TILE, :]
             stores[n].start()
 
@@ -387,10 +401,14 @@
         return carry
 
     lax.fori_loop(0, 4, corner_step, 0)
-    for r in range(6):
-        result[2, r] = (dk_acc[r + 1] * SCALE).astype(jnp.bfloat16)
-        result[3, r] = dv_acc[r + 1].astype(jnp.bfloat16)
+    def round_rows(first):
+        for r in range(3):
+            result[2, first + r] = (dk_acc[first + r + 1] * SCALE).astype(jnp.bfloat16)
+            result[3, first + r] = dv_acc[first + r + 1].astype(jnp.bfloat16)
+
+    round_rows(3 * other)
     start([result_copy(1)])
+    round_rows(3 * core)
     write(1)
     for copy in sent + lon_rows()[4:]:
         copy.wait_send()

time: 123 us -> 123 us (level)
  no operation moved by 1% of the time
where the time goes in v5:
time: 123 us
  Pallas kernels  122 us (99%)
    pallas_call x1, Pallas kernels, on_device(): pl.pallas_call(kernel, out_shape=outs, in_specs=[hbm] * 7, out_specs=[hbm...  120 us

profile of v5, /device:TPU:1, one launch (start us, length us, event | category | flops | bytes accessed | tf_op | source)
XLA Modules:
  0.0 122.6 jit_solution(10094500209923369100)
XLA Ops:
  0.6 119.9 %sphere.1 = (bf16[3,45,1024]{2,1,0:T(8,128)(2,1)}, bf16[3,45,1024]{2,1,0:T(8,128)(2,1)}, bf16[3,45,1024]{2,1,0:T(8,128)(2,1)}, bf16[3,45,1024]{2,1,0:T(8,128)(2,1)}) custom-call(bf16[3,45,1024]{2,1,0:T(8,128)(2,1)} %q_in.1, bf16[3,45,1024]{2,1,0:T(8,128)(2,1)} %k_in.1, bf16[3,45,1024]{2,1,0:T(8,128)(2,1)} %v_in.1, bf16[3,45,1024]{2,1,0:T(8,128)(2,1)} %g_in.1, ...), custom_call_target="tpu_custom_call" | custom-call | tf_op jit(solution)/shard_map/sphere/pallas_call | solution.py:440
  120.5 2.0 %finish.1 = (bf16[3,45,1024]{2,1,0:T(8,128)(2,1)}, bf16[3,45,1024]{2,1,0:T(8,128)(2,1)}, bf16[3,45,1024]{2,1,0:T(8,128)(2,1)}, bf16[3,45,1024]{2,1,0:T(8,128)(2,1)}) custom-call(bf16[3,45,1024]{2,1,0:T(8,128)(2,1)} %get-tuple-element.8.refs_0_, bf16[3,45,1024]{2,1,0:T(8,128)(2,1)} %get-tuple-element.9.refs_1_, ...), custom_call_target="tpu_custom_call" | custom-call | tf_op jit(solution)/shard_map/finish/pallas_call | solution.py:468
